TPU v7x, 512 devices: a whole 4x4x16 slice. The times are simulated.
512 devices in a mesh: expert: 16 (over x, z_lo), shard: 32 (over z_hi, y, core).
Axes of the slice: x: 4, y: 4, z: 16 (z_hi: 4, z_lo: 4; z = z_hi * 4 + z_lo), core: 2. Of those that a mesh axis runs over, the one named last changes fastest.
Arguments:
- tokens: bfloat16 [65536, 3072], P(('expert', 'shard')), may hold values from -6 to 6
- expert_ids: int32 [65536, 1], P(('expert', 'shard')), may hold values from 0 to 63, as said below
- gate_weight: bfloat16 [64, 1024, 3072], P('expert', 'shard'), may hold values from -0.109375 to 0.109375
- up_weight: bfloat16 [64, 1024, 3072], P('expert', 'shard'), may hold values from -0.109375 to 0.109375
- down_weight: bfloat16 [64, 1024, 3072], P('expert', 'shard'), may hold values from -0.1875 to 0.1875
Outputs:
- moe_output: bfloat16 [65536, 3072], P(('expert', 'shard'))
Inputs may be any that keep to these rules, and one draw needn't show every extreme that they name: `expert_ids`: among each device's 128 tokens no expert is named more than 3 times; one expert, the same on every device, is named exactly 3 times on every device.
All inputs are finite; a program needn't handle non-finite values.
Results may differ from a plain program's by a relative error of at most 0.0049.
Values may be sent and summed in bfloat16 or wider, within the bound.
No kernel may reach another device: no remote copies, remote signals or barrier semaphores. Data moves between devices by JAX's collectives and lax.ppermute only.
A program may use at most 64 MiB of HBM per device.

v0:
```python
import jax
import jax.numpy as jnp
from jax import lax
from jax.sharding import PartitionSpec as P


def partner_2(x, axis, bit):
    return lax.ppermute(x, axis, [(i, i ^ 1 << bit) for i in range(lax.axis_size(axis))])


def shards(tokens, expert_ids, gate_weight, up_weight, down_weight):
    group_count = lax.axis_size("expert")
    shard_count = lax.axis_size("shard")
    exp_dev, unit_rows, feature_width = gate_weight.shape
    sub_size = shard_count // exp_dev
    splits = min(4, sub_size)
    groups_units = sub_size // splits
    tok_rows = tokens.shape[0]
    experts_all = exp_dev * group_count
    capacity = max(2, 3 * tok_rows // (2 * experts_all))
    slice_width = feature_width // splits
    col_width = feature_width // sub_size
    unit_piece = unit_rows // groups_units
    slot_count = experts_all * capacity
    slot_total = shard_count * group_count * capacity
    flat_ids = expert_ids[:, 0]
    matches = (flat_ids[:, None] == jnp.arange(experts_all, dtype=jnp.int32)[None, :]).astype(
        jnp.int32
    )
    rank_of = jnp.sum((jnp.cumsum(matches, axis=0) - 1) * matches, axis=1)
    group_of = flat_ids // exp_dev
    local_of = flat_ids % exp_dev
    position = (group_of * capacity + rank_of) * exp_dev + local_of
    selector = (position[None, :] == jnp.arange(slot_count, dtype=jnp.int32)[:, None]).astype(
        jnp.bfloat16
    )
    packed = jnp.dot(selector, tokens, preferred_element_type=jnp.float32).astype(jnp.bfloat16)
    packed = packed.reshape(group_count, capacity, exp_dev, feature_width)

    def arrange(weight_in):
        pieces = weight_in.reshape(exp_dev, groups_units, unit_piece, splits, slice_width)
        return pieces.transpose(0, 3, 1, 2, 4).reshape(shard_count, unit_piece, slice_width)

    down_pieces = down_weight.reshape(exp_dev, unit_rows, sub_size, col_width).transpose(0, 2, 1, 3)
    down_pieces = down_pieces.reshape(shard_count, unit_rows, col_width)
    gate_in, up_in, down_in = (
        lax.all_to_all(arrange(gate_weight), "shard", split_axis=0, concat_axis=0, tiled=True),
        lax.all_to_all(arrange(up_weight), "shard", split_axis=0, concat_axis=0, tiled=True),
        lax.all_to_all(down_pieces, "shard", split_axis=0, concat_axis=0, tiled=True),
    )
    pair_weights = jnp.stack(
        [
            gate_in.reshape(shard_count * unit_piece, slice_width),
            up_in.reshape(shard_count * unit_piece, slice_width),
        ]
    )
    arrived = lax.all_to_all(packed, "expert", split_axis=0, concat_axis=0, tiled=True)
    spread = arrived.reshape(group_count, capacity, exp_dev, splits, slice_width).transpose(
        2, 3, 0, 1, 4
    )
    spread = jnp.broadcast_to(
        spread[:, :, None], (exp_dev, splits, groups_units, group_count, capacity, slice_width)
    )
    spread = spread.reshape(shard_count, group_count, capacity, slice_width)
    combined = jnp.einsum(
        "...d,pud->p...u",
        lax.all_to_all(spread, "shard", split_axis=0, concat_axis=0, tiled=True),
        pair_weights,
        preferred_element_type=jnp.float32,
    )
    combined = combined.reshape(2, slot_total, combined.shape[-1])
    my_index = lax.axis_index("shard")
    low_bits = groups_units.bit_length() - 1
    top_bits = sub_size.bit_length() - 1
    for bit_pos in range(top_bits - 1, low_bits - 1, -1):
        half_width = combined.shape[2] // 2
        my_bit = my_index >> bit_pos & 1
        kept_part = lax.dynamic_slice_in_dim(combined, my_bit * half_width, half_width, 2)
        given_part = lax.dynamic_slice_in_dim(combined, (1 - my_bit) * half_width, half_width, 2)
        combined = kept_part + partner_2(given_part, "shard", bit_pos)
    hidden = (jax.nn.silu(combined[0]) * combined[1]).astype(jnp.bfloat16)
    blocks = hidden[None]
    for bit_pos in range(top_bits):
        my_bit = my_index >> bit_pos & 1
        partner = partner_2(blocks, "shard", bit_pos)
        lower_part = jnp.where(my_bit == 1, partner, blocks)
        upper_part = jnp.where(my_bit == 1, blocks, partner)
        blocks = jnp.concatenate([lower_part, upper_part], axis=0)
    blocks = blocks.reshape(splits, groups_units, slot_total, shard_count // splits, unit_piece)
    down_local = down_in.reshape(splits, shard_count // splits, groups_units, unit_piece, col_width)
    result = jnp.einsum(
        "abnst,asbtc->nc", blocks, down_local, preferred_element_type=jnp.float32
    ).astype(jnp.bfloat16)
    result = result.reshape(shard_count, group_count, capacity, col_width)
    returned = lax.all_to_all(
        lax.all_to_all(result, "expert", split_axis=1, concat_axis=1, tiled=True),
        "shard",
        split_axis=0,
        concat_axis=3,
        tiled=True,
    )
    gathered = returned.reshape(slot_count, feature_width)
    output = lax.dot_general(
        selector, gathered, (((0,), (0,)), ((), ())), preferred_element_type=jnp.float32
    )
    return output.astype(jnp.bfloat16)


def solution(mesh):
    return jax.shard_map(
        shards,
        mesh=mesh,
        in_specs=(
            P(("expert", "shard"), None),
            P(("expert", "shard"), None),
            P("expert", "shard", None),
            P("expert", "shard", None),
            P("expert", "shard", None),
        ),
        out_specs=P(("expert", "shard"), None),
        check_vma=False,
    )
```

profile of v0, /device:TPU:65, one launch (start us, length us, event | category | flops | bytes accessed | tf_op | source)
XLA Modules:
  0.0 616.0 jit_solution(8279298541853552419)
XLA Ops:
  0.0 2.1 reshape.98
  2.1 0.0 copy-start.10
  2.1 1.0 copy.35
  3.1 16.8 %all-to-all-start = ((bf16[32,16,768]{2,1,0:T(8,128)(2,1)}), bf16[32,16,768]{2,1,0:T(8,128)(2,1)S(1)}, u32[]{:S(2)}, u32[]{:S(2)}) async-start(bf16[32,16,768]{2,1,0:T(8,128)(2,1)} %bitcast.2), calls=%async_computation | async-start | bytes 1572864 | tf_op jit(solution)/shard_map/all_to_all | solution.py:47
  19.8 0.1 fusion.8
  19.9 0.2 reduce_window_sum.11
  20.1 0.2 select_reduce_fusion
  20.3 0.5 convolution_convert_fusion
  20.8 1.3 reshape.102
  22.1 42.3 %all-to-all-done = bf16[32,16,768]{2,1,0:T(8,128)(2,1)S(1)} async-done(((bf16[32,16,768]{2,1,0:T(8,128)(2,1)}), bf16[32,16,768]{2,1,0:T(8,128)(2,1)S(1)}, u32[]{:S(2)}, u32[]{:S(2)}) %all-to-all-start) | async-done | bytes 786464 | tf_op jit(solution)/shard_map/all_to_all | solution.py:47
  64.4 6.1 all-to-all-start.2
  70.5 0.6 reshape.100
  71.1 1.0 copy.36
  72.1 24.9 %all-to-all-done.2 = bf16[16,3,4,3072]{3,2,1,0:T(4,128)(2,1)S(1)} async-done(((bf16[16,3,4,3072]{3,2,1,0:T(4,128)(2,1)}), bf16[16,3,4,3072]{3,2,1,0:T(4,128)(2,1)S(1)}, u32[]{:S(2)}, u32[]{:S(2)}) %all-to-all-start.2) | async-done | bytes 1179680 | tf_op jit(solution)/shard_map/all_to_all | solution.py:57
  97.0 5.0 all-to-all-start.1
  102.0 0.5 reshape.103
  102.5 0.3 copy.37
  102.8 29.5 %all-to-all-done.1 = bf16[32,16,768]{2,1,0:T(8,128)(2,1)S(1)} async-done(((bf16[32,16,768]{2,1,0:T(8,128)(2,1)}), bf16[32,16,768]{2,1,0:T(8,128)(2,1)S(1)}, u32[]{:S(2)}, u32[]{:S(2)}) %all-to-all-start.1) | async-done | bytes 786464 | tf_op jit(solution)/shard_map/all_to_all | solution.py:48
  132.3 1.7 broadcast_in_dim.2
  134.0 19.8 %all-to-all-start.3 = ((bf16[32,16,3,768]{3,1,2,0:T(8,128)(2,1)}), bf16[32,16,3,768]{3,1,2,0:T(8,128)(2,1)S(1)}, u32[]{:S(2)}, u32[]{:S(2)}) async-start(bf16[32,16,3,768]{3,1,2,0:T(8,128)(2,1)} %bitcast.10), calls=%async_computation.3 | async-start | bytes 4718592 | tf_op jit(solution)/shard_map/all_to_all | solution.py:67
  153.8 81.2 %all-to-all-done.3 = bf16[32,16,3,768]{3,1,2,0:T(8,128)(2,1)S(1)} async-done(((bf16[32,16,3,768]{3,1,2,0:T(8,128)(2,1)}), bf16[32,16,3,768]{3,1,2,0:T(8,128)(2,1)S(1)}, u32[]{:S(2)}, u32[]{:S(2)}) %all-to-all-start.3) | async-done | bytes 2359328 | tf_op jit(solution)/shard_map/all_to_all | solution.py:67
  235.0 5.7 convolution_bitcast_fusion.1
  240.8 10.3 %copy.39 = f32[2,32,16,3,512]{4,0,3,2,1:T(2,128)} copy(f32[2,32,16,3,512]{4,1,3,2,0:T(8,128)} %convolution_bitcast_fusion.1) | data formatting | bytes 12582912 | tf_op jit(solution)/shard_map/...d,pud->p...u/transpose | solution.py:65
  251.0 4.9 constant_dynamic-slice_fusion
  256.0 8.8 %collective-permute-start = (f32[2,1536,256]{2,0,1:T(2,128)}, f32[2,1536,256]{2,0,1:T(2,128)}, u32[]{:S(2)}, u32[]{:S(2)}) collective-permute-start(f32[2,1536,256]{2,0,1:T(2,128)} %constant_dynamic-slice_fusion), channel_id=1, source_target_pairs={{0,4},{1,5},{2,6},{3,7},{4,0},{5,1},{6,2},{7,3},{8,12},{9,13},{10,... | collective-permute-start | bytes 9437192 | tf_op jit(solution)/shard_map/ppermute | solution.py:8
  264.8 42.0 %collective-permute-done = f32[2,1536,256]{2,0,1:T(2,128)} collective-permute-done((f32[2,1536,256]{2,0,1:T(2,128)}, f32[2,1536,256]{2,0,1:T(2,128)}, u32[]{:S(2)}, u32[]{:S(2)}) %collective-permute-start) | collective-permute-done | bytes 3145760 | tf_op jit(solution)/shard_map/ppermute | solution.py:8
  306.8 4.2 dynamic-slice_add_fusion
  311.0 0.6 constant_dynamic-slice_fusion.1
  311.6 1.0 copy-done.2
  312.7 24.6 %collective-permute-start.1 = (f32[2,1536,128]{2,0,1:T(2,128)S(1)}, f32[2,1536,128]{2,0,1:T(2,128)}, u32[]{:S(2)}, u32[]{:S(2)}) collective-permute-start(f32[2,1536,128]{2,0,1:T(2,128)S(1)} %constant_dynamic-slice_fusion.1), channel_id=1, source_target_pairs={{0,2},{1,3},{2,0},{3,1},{4,6},{5,7},{6,4},{7,5},{8,10},{9,11},{10,... | collective-permute-start | bytes 4718600 | tf_op jit(solution)/shard_map/ppermute | solution.py:8
  337.3 29.4 %collective-permute-done.1 = f32[2,1536,128]{2,0,1:T(2,128)} collective-permute-done((f32[2,1536,128]{2,0,1:T(2,128)S(1)}, f32[2,1536,128]{2,0,1:T(2,128)}, u32[]{:S(2)}, u32[]{:S(2)}) %collective-permute-start.1) | collective-permute-done | bytes 1572896 | tf_op jit(solution)/shard_map/ppermute | solution.py:8
  366.7 2.3 dynamic-slice_add_fusion.1
  369.0 1.9 fusion.7
  370.9 0.1 copy.40
  370.9 7.9 %collective-permute-start.2 = (bf16[1,1536,128]{2,1,0:T(8,128)(2,1)S(1)}, bf16[1,1536,128]{2,1,0:T(8,128)(2,1)S(1)}, u32[]{:S(2)}, u32[]{:S(2)}) collective-permute-start(bf16[1,1536,128]{2,1,0:T(8,128)(2,1)S(1)} %copy.40), channel_id=1, source_target_pairs={{0,1},{1,0},{2,3},{3,2},{4,5},{5,4},{6,7},{7,6},{8,9},{9,8},{10,11... | collective-permute-start | bytes 1179656 | tf_op jit(solution)/shard_map/ppermute | solution.py:8
  378.8 1.3 collective-permute-done.2
  380.2 6.5 %broadcast_select_fusion.1 = (bf16[1,1536,128]{2,0,1:T(2,128)(2,1)S(1)}, bf16[1,1536,128]{2,0,1:T(2,128)(2,1)S(1)}) fusion(pred[]{:T(512)S(6)} %eq.48, bf16[1,1536,128]{2,1,0:T(8,128)(2,1)S(1)} %collective-permute-done.2, f32[2,1536,128]{2,0,1:T(2,128)S(1)} %dynamic-slice_add_fusion.1), kind=kLoop, calls=%fused_computation.15 | loop fusion | flops 1572864 | bytes 2752513 | tf_op jit(solution)/shard_map/jit(_where)/select_n | solution.py:86
  386.7 0.0 copy-start.3
  386.7 0.0 copy-start.6
  386.7 1.8 pad_maximum_fusion.2
  388.5 3.4 collective-permute-start.3
  391.9 0.1 copy.51
  392.1 0.1 bitcast_bitcast_fusion
  392.2 0.0 copy-start.4
  392.2 1.0 copy.44
  393.2 36.2 %all-to-all-start.4 = ((bf16[32,32,384]{2,1,0:T(8,128)(2,1)}), bf16[32,32,384]{2,1,0:T(8,128)(2,1)}, u32[]{:S(2)}, u32[]{:S(2)}) async-start(bf16[32,32,384]{2,1,0:T(8,128)(2,1)} %bitcast.16), calls=%async_computation.4 | async-start | bytes 1572864 | tf_op jit(solution)/shard_map/all_to_all | solution.py:49
  429.4 0.0 collective-permute-done.3
  429.4 3.5 broadcast_select_fusion.3
  432.9 2.6 pad_maximum_fusion.1
  435.5 5.0 collective-permute-start.4
  440.5 39.1 %collective-permute-done.4 = bf16[4,1536,128]{2,0,1:T(4,128)(2,1)} collective-permute-done((bf16[4,1536,128]{2,0,1:T(4,128)(2,1)}, bf16[4,1536,128]{2,0,1:T(4,128)(2,1)}, u32[]{:S(2)}, u32[]{:S(2)}) %collective-permute-start.4) | collective-permute-done | bytes 1572896 | tf_op jit(solution)/shard_map/ppermute | solution.py:8
  479.6 3.6 broadcast_select_fusion.5
  483.3 2.8 pad_maximum_fusion
  486.1 5.0 copy.43
  491.1 3.9 fusion
  495.0 0.6 reshape.110
  495.7 0.9 copy.46
  496.6 42.7 %all_to_all.45 = bf16[32,16,3,384]{3,0,2,1:T(8,128)(2,1)S(1)} all-to-all(bf16[32,16,3,384]{3,0,2,1:T(8,128)(2,1)S(1)} %copy.46), channel_id=1, replica_groups=mesh['expert'=16,'shard'=32] {'expert'}, dimensions={1} | all-to-all | bytes 2359296 | tf_op jit(solution)/shard_map/all_to_all | solution.py:96
  539.3 0.4 copy.47
  539.7 74.2 %all_to_all.46 = bf16[32,16,3,384]{3,1,2,0:T(8,128)(2,1)S(1)} all-to-all(bf16[32,16,3,384]{3,1,2,0:T(8,128)(2,1)S(1)} %copy.47), channel_id=1, replica_groups=mesh['expert'=16,'shard'=32] {'shard'}, dimensions={0} | all-to-all | bytes 2359296 | tf_op jit(solution)/shard_map/all_to_all | solution.py:95
  613.9 0.2 copy.48
  614.1 0.0 copy-start.1
  614.1 0.6 reshape.111
  614.7 1.3 convolution_convert_fusion.1
  (18 shorter events, 0.1 us)
Async XLA Ops:
  0.0 20.3 %copy-start = (bf16[128,3072]{1,0:T(8,128)(2,1)S(1)}, bf16[128,3072]{1,0:T(8,128)(2,1)}, u32[]{:S(2)}) copy-start(bf16[128,3072]{1,0:T(8,128)(2,1)} %param.5) | copy-start | bytes 2359300
  2.1 17.8 %copy-start.10 = (s32[128,1]{0,1:T(1,128)S(1)}, s32[128,1]{0,1:T(1,128)}, u32[]{:S(2)}) copy-start(s32[128,1]{0,1:T(1,128)} %param.6) | copy-start | bytes 1540
  3.1 61.3 %all-to-all-start = ((bf16[32,16,768]{2,1,0:T(8,128)(2,1)}), bf16[32,16,768]{2,1,0:T(8,128)(2,1)S(1)}, u32[]{:S(2)}, u32[]{:S(2)}) async-start(bf16[32,16,768]{2,1,0:T(8,128)(2,1)} %bitcast.2), calls=%async_computation | async-start | bytes 1572864 | tf_op jit(solution)/shard_map/all_to_all | solution.py:47
  22.1 48.4 %copy-start.5 = (bf16[4,32,3072]{2,1,0:T(8,128)(2,1)S(1)}, bf16[4,32,3072]{2,1,0:T(8,128)(2,1)}, u32[]{:S(2)}) copy-start(bf16[4,32,3072]{2,1,0:T(8,128)(2,1)} %param.8) | copy-start | bytes 2359300
  64.4 6.7 %copy-start.7 = (bf16[32,16,768]{2,1,0:T(8,128)(2,1)}, bf16[32,16,768]{2,1,0:T(8,128)(2,1)S(1)}, u32[]{:S(2)}) copy-start(bf16[32,16,768]{2,1,0:T(8,128)(2,1)S(1)} %all-to-all-done) | copy-start | bytes 2359300
  64.4 32.6 %all-to-all-start.2 = ((bf16[16,3,4,3072]{3,2,1,0:T(4,128)(2,1)}), bf16[16,3,4,3072]{3,2,1,0:T(4,128)(2,1)S(1)}, u32[]{:S(2)}, u32[]{:S(2)}) async-start(bf16[16,3,4,3072]{3,2,1,0:T(4,128)(2,1)} %reshape.102), calls=%async_computation.2 | async-start | bytes 2359296 | tf_op jit(solution)/shard_map/all_to_all | solution.py:57
  97.0 35.3 %all-to-all-start.1 = ((bf16[32,16,768]{2,1,0:T(8,128)(2,1)}), bf16[32,16,768]{2,1,0:T(8,128)(2,1)S(1)}, u32[]{:S(2)}, u32[]{:S(2)}) async-start(bf16[32,16,768]{2,1,0:T(8,128)(2,1)} %bitcast.5), calls=%async_computation.1 | async-start | bytes 1572864 | tf_op jit(solution)/shard_map/all_to_all | solution.py:48
  132.3 1.7 copy-start.9
  134.0 101.1 %copy-start.8 = (bf16[32,16,768]{2,1,0:T(8,128)(2,1)S(1)}, bf16[32,16,768]{2,1,0:T(8,128)(2,1)}, u32[]{:S(2)}) copy-start(bf16[32,16,768]{2,1,0:T(8,128)(2,1)} %copy-done.7) | copy-start | bytes 2359300
  134.0 101.0 %all-to-all-start.3 = ((bf16[32,16,3,768]{3,1,2,0:T(8,128)(2,1)}), bf16[32,16,3,768]{3,1,2,0:T(8,128)(2,1)S(1)}, u32[]{:S(2)}, u32[]{:S(2)}) async-start(bf16[32,16,3,768]{3,1,2,0:T(8,128)(2,1)} %bitcast.10), calls=%async_computation.3 | async-start | bytes 4718592 | tf_op jit(solution)/shard_map/all_to_all | solution.py:67
  256.0 50.8 %collective-permute-start = (f32[2,1536,256]{2,0,1:T(2,128)}, f32[2,1536,256]{2,0,1:T(2,128)}, u32[]{:S(2)}, u32[]{:S(2)}) collective-permute-start(f32[2,1536,256]{2,0,1:T(2,128)} %constant_dynamic-slice_fusion), channel_id=1, source_target_pairs={{0,4},{1,5},{2,6},{3,7},{4,0},{5,1},{6,2},{7,3},{8,12},{9,13},{10,... | collective-permute-start | bytes 9437192 | tf_op jit(solution)/shard_map/ppermute | solution.py:8
  311.0 1.6 copy-start.2
  312.7 54.0 %collective-permute-start.1 = (f32[2,1536,128]{2,0,1:T(2,128)S(1)}, f32[2,1536,128]{2,0,1:T(2,128)}, u32[]{:S(2)}, u32[]{:S(2)}) collective-permute-start(f32[2,1536,128]{2,0,1:T(2,128)S(1)} %constant_dynamic-slice_fusion.1), channel_id=1, source_target_pairs={{0,2},{1,3},{2,0},{3,1},{4,6},{5,7},{6,4},{7,5},{8,10},{9,11},{10,... | collective-permute-start | bytes 4718600 | tf_op jit(solution)/shard_map/ppermute | solution.py:8
  370.9 9.2 %collective-permute-start.2 = (bf16[1,1536,128]{2,1,0:T(8,128)(2,1)S(1)}, bf16[1,1536,128]{2,1,0:T(8,128)(2,1)S(1)}, u32[]{:S(2)}, u32[]{:S(2)}) collective-permute-start(bf16[1,1536,128]{2,1,0:T(8,128)(2,1)S(1)} %copy.40), channel_id=1, source_target_pairs={{0,1},{1,0},{2,3},{3,2},{4,5},{5,4},{6,7},{7,6},{8,9},{9,8},{10,11... | collective-permute-start | bytes 1179656 | tf_op jit(solution)/shard_map/ppermute | solution.py:8
  386.7 5.4 copy-start.3
  386.7 5.2 copy-start.6
  388.5 40.9 %collective-permute-start.3 = (bf16[2,1536,128]{2,0,1:T(2,128)(2,1)S(1)}, bf16[2,1536,128]{2,0,1:T(2,128)(2,1)}, u32[]{:S(2)}, u32[]{:S(2)}) collective-permute-start(bf16[2,1536,128]{2,0,1:T(2,128)(2,1)S(1)} %pad_maximum_fusion.2), channel_id=1, source_target_pairs={{0,2},{1,3},{2,0},{3,1},{4,6},{5,7},{6,4},{7,5},{8,10},{9,11},{10,... | collective-permute-start | bytes 2359304 | tf_op jit(solution)/shard_map/ppermute | solution.py:8
  392.2 37.3 %copy-start.4 = (bf16[1,1536,128]{2,0,1:T(2,128)(2,1)S(1)}, bf16[1,1536,128]{2,0,1:T(2,128)(2,1)}, u32[]{:S(2)}) copy-start(bf16[1,1536,128]{2,0,1:T(2,128)(2,1)} %copy-done.3) | copy-start | bytes 1179652
  393.2 98.0 %all-to-all-start.4 = ((bf16[32,32,384]{2,1,0:T(8,128)(2,1)}), bf16[32,32,384]{2,1,0:T(8,128)(2,1)}, u32[]{:S(2)}, u32[]{:S(2)}) async-start(bf16[32,32,384]{2,1,0:T(8,128)(2,1)} %bitcast.16), calls=%async_computation.4 | async-start | bytes 1572864 | tf_op jit(solution)/shard_map/all_to_all | solution.py:49
  435.5 44.2 %collective-permute-start.4 = (bf16[4,1536,128]{2,0,1:T(4,128)(2,1)}, bf16[4,1536,128]{2,0,1:T(4,128)(2,1)}, u32[]{:S(2)}, u32[]{:S(2)}) collective-permute-start(bf16[4,1536,128]{2,0,1:T(4,128)(2,1)} %pad_maximum_fusion.1), channel_id=1, source_target_pairs={{0,4},{1,5},{2,6},{3,7},{4,0},{5,1},{6,2},{7,3},{8,12},{9,13},{10,... | collective-permute-start | bytes 4718600 | tf_op jit(solution)/shard_map/ppermute | solution.py:8
  614.1 1.9 copy-start.1
where the time goes:
time: 617 us; the launch traced here: 616 us
  waiting for transfers between devices  290 us (47%)
  starting transfers between devices  134 us (22%)
  blocking collectives  117 us (19%)
  local copies, waits for them, and re-layouts  34.3 us (6%)
  other arithmetic  29.6 us (5%)
  matrix products  11.4 us (2%)
    ppermute x5, waiting for transfers between devices, partner_2(): lax.ppermute(x, axis, [(i, i ^ 1 << bit) for i in range(lax.axis_size(axi...  112 us
    all_to_all x1, waiting for transfers between devices, shards(): lax.all_to_all(spread, 'shard', split_axis=0, concat_axis=0, tiled=True)  81.2 us
    all_to_all x1, blocking collectives, shards(): lax.all_to_all(lax.all_to_all(result, 'expert', split_axis=1, concat_axis...  74.2 us
    ppermute x5, starting transfers between devices, partner_2(): lax.ppermute(x, axis, [(i, i ^ 1 << bit) for i in range(lax.axis_size(axi...  49.7 us
    all_to_all x1, blocking collectives, shards(): lax.all_to_all(result, 'expert', split_axis=1, concat_axis=1, tiled=True)  42.7 us
    all_to_all x1, waiting for transfers between devices, shards(): lax.all_to_all(arrange(gate_weight), 'shard', split_axis=0, concat_axis=0...  42.3 us
    all_to_all x1, starting transfers between devices, shards(): lax.all_to_all(down_pieces, 'shard', split_axis=0, concat_axis=0, tiled=T...  36.2 us
    all_to_all x1, waiting for transfers between devices, shards(): lax.all_to_all(arrange(up_weight), 'shard', split_axis=0, concat_axis=0,...  29.5 us
  transfers between devices with their start and end apart: 10, of which 8 were waited for; matrix products, arithmetic and copies ran while one was open for 4% of the time, Pallas kernels for 0%

commit v1 on v0

v1 whole, which is shorter than its diff:
```python
import jax
import jax.numpy as jnp
from jax import lax
from jax.sharding import Mesh, PartitionSpec as P

CAP = 3
CHUNKS = 8


def shards(tokens, expert_ids, gate_weight, up_weight, down_weight):
    exp_dev, unit_rows, width = gate_weight.shape
    rows = tokens.shape[0]
    routes = ("x", "zlo", "zhi")
    plane = ("y", "core")
    experts = exp_dev * lax.axis_size("x") * lax.axis_size("zlo")
    chunk = width // CHUNKS
    slots = experts * CAP

    def owned(weight):
        part = lax.all_to_all(weight, "zhi", split_axis=0, concat_axis=0, tiled=True)
        return lax.all_gather(part, plane, axis=0, tiled=True).reshape(-1, width)

    gate_full = owned(gate_weight)
    up_full = owned(up_weight)
    down_full = owned(down_weight)

    flat_ids = expert_ids[:, 0]
    matches = (flat_ids[:, None] == jnp.arange(experts, dtype=jnp.int32)[None, :]).astype(jnp.int32)
    rank_of = jnp.sum((jnp.cumsum(matches, axis=0) - 1) * matches, axis=1)
    position = flat_ids * CAP + rank_of
    selector = (position[None, :] == jnp.arange(slots, dtype=jnp.int32)[:, None]).astype(jnp.bfloat16)
    packed = jnp.dot(selector, tokens, preferred_element_type=jnp.float32).astype(jnp.bfloat16)
    packed = packed.reshape(experts, CAP * CHUNKS, chunk)
    arrived = lax.all_to_all(packed, routes, split_axis=0, concat_axis=0, tiled=True)
    arrived = arrived.reshape(slots, width)
    gate_value = lax.dot_general(
        arrived, gate_full, (((1,), (1,)), ((), ())), preferred_element_type=jnp.float32
    )
    up_value = lax.dot_general(
        arrived, up_full, (((1,), (1,)), ((), ())), preferred_element_type=jnp.float32
    )
    hidden = (jax.nn.silu(gate_value) * up_value).astype(jnp.bfloat16)
    result = jnp.dot(hidden, down_full, preferred_element_type=jnp.float32).astype(jnp.bfloat16)
    result = result.reshape(experts, CAP * CHUNKS, chunk)
    returned = lax.all_to_all(result, routes, split_axis=0, concat_axis=0, tiled=True)
    returned = returned.reshape(slots, width)
    output = lax.dot_general(
        selector, returned, (((0,), (0,)), ((), ())), preferred_element_type=jnp.float32
    )
    return output.astype(jnp.bfloat16)


def solution(mesh):
    fine = Mesh(mesh.devices.reshape(4, 4, 4, 4, 2), ("x", "zlo", "zhi", "y", "core"))
    everyone = ("x", "zlo", "zhi", "y", "core")
    group = ("x", "zlo")
    sub = ("zhi", "y", "core")
    return jax.shard_map(
        shards,
        mesh=fine,
        in_specs=(
            P(everyone, None),
            P(everyone, None),
            P(group, sub, None),
            P(group, sub, None),
            P(group, sub, None),
        ),
        out_specs=P(everyone, None),
        check_vma=False,
    )
```

time: 617 us -> 306 us (0.50)
  the two profiles are of different devices: /device:TPU:65 before, /device:TPU:56 now
where the time goes in v1:
time: 306 us
  blocking collectives  274 us (90%)
  matrix products  16.1 us (5%)
  between operations  13.2 us (4%)
    all_to_all x3, blocking collectives, owned(): lax.all_to_all(weight, 'zhi', split_axis=0, concat_axis=0, tiled=True)  141 us
    all_to_all x1, blocking collectives, shards(): lax.all_to_all(packed, routes, split_axis=0, concat_axis=0, tiled=True)  67.4 us
    all_to_all x1, blocking collectives, shards(): lax.all_to_all(result, routes, split_axis=0, concat_axis=0, tiled=True)  65.6 us
    dot_general x1, matrix products, shards(): jnp.dot(hidden, down_full, preferred_element_type=jnp.float32)  8.37 us
  transfers between devices with their start and end apart: 3, of which 0 were waited for; matrix products, arithmetic and copies ran while one was open for 3% of the time, Pallas kernels for 0%

profile of v1, /device:TPU:56, one launch (start us, length us, event | category | flops | bytes accessed | tf_op | source)
XLA Modules:
  0.0 305.9 jit_solution(13475321276541084147)
XLA Ops:
  6.5 0.0 copy-start
  6.5 0.0 copy-start.1
  6.5 0.0 all-gather.4.cloned.1.call-start
  6.5 58.3 %all_to_all.25 = bf16[4,32,3072]{2,1,0:T(8,128)(2,1)} all-to-all(bf16[4,32,3072]{2,1,0:T(8,128)(2,1)} %param.7), channel_id=1, replica_groups=mesh['x'=4,'zlo'=4,'zhi'=4,'y'=4,'core'=2] {'zhi'}, dimensions={0} | all-to-all | bytes 1572864 | tf_op jit(solution)/shard_map/all_to_all | solution.py:20
  64.8 0.0 all-gather.4.cloned.1.call-update
  64.8 0.0 copy-start.2
  64.8 0.0 all-gather.6.cloned.1.call-start
  64.9 0.0 copy-done.1
  64.9 44.7 %all_to_all.26 = bf16[4,32,3072]{2,1,0:T(8,128)(2,1)} all-to-all(bf16[4,32,3072]{2,1,0:T(8,128)(2,1)S(1)} %copy-done.1), channel_id=1, replica_groups=mesh['x'=4,'zlo'=4,'zhi'=4,'y'=4,'core'=2] {'zhi'}, dimensions={0} | all-to-all | bytes 1572864 | tf_op jit(solution)/shard_map/all_to_all | solution.py:20
  109.6 0.0 all-gather.6.cloned.1.call-update
  109.7 0.0 copy-start.3
  109.7 0.0 all-gather.8.cloned.1.call-start
  109.7 0.0 copy-done.2
  109.7 37.8 %all_to_all.27 = bf16[4,32,3072]{2,1,0:T(8,128)(2,1)} all-to-all(bf16[4,32,3072]{2,1,0:T(8,128)(2,1)S(1)} %copy-done.2), channel_id=1, replica_groups=mesh['x'=4,'zlo'=4,'zhi'=4,'y'=4,'core'=2] {'zhi'}, dimensions={0} | all-to-all | bytes 1572864 | tf_op jit(solution)/shard_map/all_to_all | solution.py:20
  147.5 0.0 all-gather.8.cloned.1.call-update
  147.6 0.0 copy-done.3
  147.6 0.1 fusion.2
  147.7 0.2 reduce_window_sum.11
  147.8 0.2 select_reduce_fusion
  148.0 0.0 copy-done
  148.0 0.5 convolution_convert_fusion.1
  148.5 0.6 reshape.29
  149.1 67.4 %all_to_all.28 = bf16[64,24,384]{2,1,0:T(8,128)(2,1)S(1)} all-to-all(bf16[64,24,384]{2,1,0:T(8,128)(2,1)S(1)} %reshape.29), channel_id=1, replica_groups=mesh['x'=4,'zlo'=4,'zhi'=4,'y'=4,'core'=2] {'x','zlo','zhi'}, dimensions={0} | all-to-all | bytes 2359296 | tf_op jit(solution)/shard_map/all_to_all | solution.py:34
  216.4 0.6 reshape.30
  217.0 0.0 all-gather.4.cloned.1.call-done
  217.0 5.9 %fusion.6 = f32[192,1024]{1,0:T(8,128)} fusion(bf16[192,3072]{1,0:T(8,128)(2,1)S(1)} %reshape.30, bf16[1024,3072]{1,0:T(8,128)(2,1)} %bitcast.14), kind=kOutput, calls=%fused_computation.14 | convolution fusion | flops 1207959552 | bytes 8257536 | tf_op jit(solution)/shard_map/dot_general | solution.py:36
  223.0 0.0 all-gather.6.cloned.1.call-done
  223.0 0.0 all-gather.8.cloned.1.call-done
  223.0 8.4 %convolution_convert_fusion = bf16[192,3072]{1,0:T(8,128)(2,1)S(1)} fusion(bf16[1024,3072]{1,0:T(8,128)(2,1)} %bitcast.16, bf16[192,3072]{1,0:T(8,128)(2,1)S(1)} %reshape.30, bf16[1024,3072]{1,0:T(8,128)(2,1)} %bitcast.15, f32[192,1024]{1,0:T(8,128)} %fusion.6), kind=kOutput, calls=%fused_computation | convolution fusion | flops 2417688576 | bytes 15728640 | tf_op jit(solution)/shard_map/dot_general | solution.py:43
  231.3 0.6 reshape.34
  231.9 65.6 %all_to_all.29 = bf16[64,24,384]{2,1,0:T(8,128)(2,1)S(1)} all-to-all(bf16[64,24,384]{2,1,0:T(8,128)(2,1)S(1)} %reshape.34), channel_id=1, replica_groups=mesh['x'=4,'zlo'=4,'zhi'=4,'y'=4,'core'=2] {'x','zlo','zhi'}, dimensions={0} | all-to-all | bytes 2359296 | tf_op jit(solution)/shard_map/all_to_all | solution.py:45
  297.5 0.6 reshape.35
  298.1 1.3 convolution_convert_fusion.2
  (1 shorter events, 0.0 us)
Async XLA Ops:
  6.5 141.5 %copy-start = (bf16[128,3072]{1,0:T(8,128)(2,1)S(1)}, bf16[128,3072]{1,0:T(8,128)(2,1)}, u32[]{:S(2)}) copy-start(bf16[128,3072]{1,0:T(8,128)(2,1)} %param.5) | copy-start | bytes 2359300
  6.5 58.3 %copy-start.1 = (bf16[4,32,3072]{2,1,0:T(8,128)(2,1)S(1)}, bf16[4,32,3072]{2,1,0:T(8,128)(2,1)}, u32[]{:S(2)}) copy-start(bf16[4,32,3072]{2,1,0:T(8,128)(2,1)} %param.8) | copy-start | bytes 2359300
  6.5 210.5 %all-gather.4.cloned.1.call-start = ((), (), s32[]{:S(2)}) async-start(), calls=%async_computation.5 | async-start | bytes 7077888 | tf_op jit(solution)/shard_map/all_gather | solution.py:21
  64.8 44.9 %copy-start.2 = (bf16[4,32,3072]{2,1,0:T(8,128)(2,1)S(1)}, bf16[4,32,3072]{2,1,0:T(8,128)(2,1)}, u32[]{:S(2)}) copy-start(bf16[4,32,3072]{2,1,0:T(8,128)(2,1)} %param.9) | copy-start | bytes 2359300
  64.8 158.1 %all-gather.6.cloned.1.call-start = ((), (), s32[]{:S(2)}) async-start(), calls=%async_computation.6 | async-start | bytes 7077888 | tf_op jit(solution)/shard_map/all_gather | solution.py:21
  109.7 37.9 %copy-start.3 = (s32[128,1]{0,1:T(1,128)S(1)}, s32[128,1]{0,1:T(1,128)}, u32[]{:S(2)}) copy-start(s32[128,1]{0,1:T(1,128)} %param.6) | copy-start | bytes 1540
  109.7 113.3 %all-gather.8.cloned.1.call-start = ((), (), s32[]{:S(2)}) async-start(), calls=%async_computation.7 | async-start | bytes 7077888 | tf_op jit(solution)/shard_map/all_gather | solution.py:21
Sparse Core Ops, SparseCore 0:
  64.9 39.1 all-gather.3
  109.8 45.1 all-gather.5
  157.1 48.7 all-gather.7

commit v2 on v1

--- a/solution.py
+++ b/solution.py
@@ -16,13 +16,32 @@
     chunk = width // CHUNKS
     slots = experts * CAP
 
-    def owned(weight):
-        part = lax.all_to_all(weight, "zhi", split_axis=0, concat_axis=0, tiled=True)
-        return lax.all_gather(part, plane, axis=0, tiled=True).reshape(-1, width)
+    ring = lax.axis_size("zhi")
+    place = lax.axis_index("zhi")
 
-    gate_full = owned(gate_weight)
-    up_full = owned(up_weight)
-    down_full = owned(down_weight)
+    def piece(weight, step):
+        return lax.dynamic_slice_in_dim(weight, lax.rem(place + step, ring), 1, 0)
+
+    def passed(value, step):
+        return lax.ppermute(value, "zhi", [(i, (i + step) % ring) for i in range(ring)])
+
+    held = []
+    previous = None
+    for weight in (gate_weight, up_weight, down_weight):
+        outgoing = [piece(weight, step) for step in range(ring)]
+        if previous is not None:
+            for step in range(1, ring):
+                outgoing[step], previous[step] = lax.optimization_barrier(
+                    (outgoing[step], previous[step])
+                )
+            held[-1] = previous
+        previous = [outgoing[0]] + [passed(outgoing[step], step) for step in range(1, ring)]
+        held.append(previous)
+    own = [jnp.concatenate(pieces, axis=0) for pieces in held]
+    tokens, own[2] = lax.optimization_barrier((tokens, own[2]))
+    gate_full, up_full, down_full = (
+        lax.all_gather(part, plane, axis=0, tiled=True).reshape(-1, width) for part in own
+    )
 
     flat_ids = expert_ids[:, 0]
     matches = (flat_ids[:, None] == jnp.arange(experts, dtype=jnp.int32)[None, :]).astype(jnp.int32)
@@ -40,6 +59,7 @@
         arrived, up_full, (((1,), (1,)), ((), ())), preferred_element_type=jnp.float32
     )
     hidden = (jax.nn.silu(gate_value) * up_value).astype(jnp.bfloat16)
+    hidden = lax.optimization_barrier(hidden)
     result = jnp.dot(hidden, down_full, preferred_element_type=jnp.float32).astype(jnp.bfloat16)
     result = result.reshape(experts, CAP * CHUNKS, chunk)
     returned = lax.all_to_all(result, routes, split_axis=0, concat_axis=0, tiled=True)

time: 306 us -> 305 us (level)
  the two profiles are of different devices: /device:TPU:56 before, /device:TPU:40 now
where the time goes in v2:
time: 305 us
  blocking collectives  144 us (47%)
  starting transfers between devices  62.7 us (21%)
  waiting for transfers between devices  60.8 us (20%)
  matrix products  16.1 us (5%)
  between operations  13.3 us (4%)
  local copies, waits for them, and re-layouts  3.83 us (1%)
  other arithmetic  3.38 us (1%)
    all_to_all x1, blocking collectives, shards(): lax.all_to_all(packed, routes, split_axis=0, concat_axis=0, tiled=True)  78.8 us
    all_to_all x1, blocking collectives, shards(): lax.all_to_all(result, routes, split_axis=0, concat_axis=0, tiled=True)  65.6 us
    ppermute x9, starting transfers between devices, passed(): lax.ppermute(value, 'zhi', [(i, (i + step) % ring) for i in range(ring)])  62.6 us
    ppermute x9, waiting for transfers between devices, passed(): lax.ppermute(value, 'zhi', [(i, (i + step) % ring) for i in range(ring)])  60.7 us
  transfers between devices with their start and end apart: 12, of which 7 were waited for; matrix products, arithmetic and copies ran while one was open for 5% of the time, Pallas kernels for 0%

profile of v2, /device:TPU:40, one launch (start us, length us, event | category | flops | bytes accessed | tf_op | source)
XLA Modules:
  0.0 304.6 jit_solution(15195229957918796431)
XLA Ops:
  6.5 0.0 copy-start
  6.5 0.0 copy-start.1
  6.5 0.0 all-gather.4.cloned.1.call-start
  6.5 1.4 constant_dynamic-slice_fusion
  7.9 9.1 %collective-permute-start = (bf16[1,32,3072]{2,1,0:T(8,128)(2,1)S(1)}, bf16[1,32,3072]{2,1,0:T(8,128)(2,1)S(1)}, u32[]{:S(2)}, u32[]{:S(2)}) collective-permute-start(bf16[1,32,3072]{2,1,0:T(8,128)(2,1)S(1)} %get-tuple-element.35), channel_id=1, source_target_pairs={{0,8},{8,16},{16,24},{24,0},{1,9},{9,17},{17,25},{25,1},{2,10},{10... | collective-permute-start | bytes 589832 | tf_op jit(solution)/shard_map/ppermute | solution.py:26
  17.0 10.0 %collective-permute-start.3 = (bf16[1,32,3072]{2,1,0:T(8,128)(2,1)S(1)}, bf16[1,32,3072]{2,1,0:T(8,128)(2,1)S(1)}, u32[]{:S(2)}, u32[]{:S(2)}) collective-permute-start(bf16[1,32,3072]{2,1,0:T(8,128)(2,1)S(1)} %get-tuple-element.34), channel_id=1, source_target_pairs={{0,16},{8,24},{16,0},{24,8},{1,17},{9,25},{17,1},{25,9},{2,18},{10... | collective-permute-start | bytes 589832 | tf_op jit(solution)/shard_map/ppermute | solution.py:26
  27.1 5.5 %collective-permute-start.6 = (bf16[1,32,3072]{2,1,0:T(8,128)(2,1)S(1)}, bf16[1,32,3072]{2,1,0:T(8,128)(2,1)S(1)}, u32[]{:S(2)}, u32[]{:S(2)}) collective-permute-start(bf16[1,32,3072]{2,1,0:T(8,128)(2,1)S(1)} %get-tuple-element.36), channel_id=1, source_target_pairs={{0,24},{8,0},{16,8},{24,16},{1,25},{9,1},{17,9},{25,17},{2,26},{10... | collective-permute-start | bytes 589832 | tf_op jit(solution)/shard_map/ppermute | solution.py:26
  32.5 0.0 copy-done.1
  32.5 0.1 constant_dynamic-slice_fusion.11
  32.6 1.6 collective-permute-done
  34.2 8.8 %collective-permute-done.3 = bf16[1,32,3072]{2,1,0:T(8,128)(2,1)S(1)} collective-permute-done((bf16[1,32,3072]{2,1,0:T(8,128)(2,1)S(1)}, bf16[1,32,3072]{2,1,0:T(8,128)(2,1)S(1)}, u32[]{:S(2)}, u32[]{:S(2)}) %collective-permute-start.3) | collective-permute-done | bytes 196640 | tf_op jit(solution)/shard_map/ppermute | solution.py:26
  43.0 9.4 %collective-permute-done.6 = bf16[1,32,3072]{2,1,0:T(8,128)(2,1)S(1)} collective-permute-done((bf16[1,32,3072]{2,1,0:T(8,128)(2,1)S(1)}, bf16[1,32,3072]{2,1,0:T(8,128)(2,1)S(1)}, u32[]{:S(2)}, u32[]{:S(2)}) %collective-permute-start.6) | collective-permute-done | bytes 196640 | tf_op jit(solution)/shard_map/ppermute | solution.py:26
  52.4 0.0 copy-start.2
  52.4 1.0 pad_maximum_fusion.1
  53.4 0.0 all-gather.4.cloned.1.call-update
  53.4 0.0 all-gather.6.cloned.1.call-start
  53.5 3.3 %collective-permute-start.1 = (bf16[1,32,3072]{2,1,0:T(8,128)(2,1)S(1)}, bf16[1,32,3072]{2,1,0:T(8,128)(2,1)S(1)}, u32[]{:S(2)}, u32[]{:S(2)}) collective-permute-start(bf16[1,32,3072]{2,1,0:T(8,128)(2,1)S(1)} %get-tuple-element.19), channel_id=1, source_target_pairs={{0,8},{8,16},{16,24},{24,0},{1,9},{9,17},{17,25},{25,1},{2,10},{10... | collective-permute-start | bytes 589832 | tf_op jit(solution)/shard_map/ppermute | solution.py:26
  56.8 11.3 %collective-permute-start.4 = (bf16[1,32,3072]{2,1,0:T(8,128)(2,1)S(1)}, bf16[1,32,3072]{2,1,0:T(8,128)(2,1)S(1)}, u32[]{:S(2)}, u32[]{:S(2)}) collective-permute-start(bf16[1,32,3072]{2,1,0:T(8,128)(2,1)S(1)} %get-tuple-element.21), channel_id=1, source_target_pairs={{0,16},{8,24},{16,0},{24,8},{1,17},{9,25},{17,1},{25,9},{2,18},{10... | collective-permute-start | bytes 589832 | tf_op jit(solution)/shard_map/ppermute | solution.py:26
  68.1 6.4 %collective-permute-start.7 = (bf16[1,32,3072]{2,1,0:T(8,128)(2,1)S(1)}, bf16[1,32,3072]{2,1,0:T(8,128)(2,1)S(1)}, u32[]{:S(2)}, u32[]{:S(2)}) collective-permute-start(bf16[1,32,3072]{2,1,0:T(8,128)(2,1)S(1)} %get-tuple-element.23), channel_id=1, source_target_pairs={{0,24},{8,0},{16,8},{24,16},{1,25},{9,1},{17,9},{25,17},{2,26},{10... | collective-permute-start | bytes 589832 | tf_op jit(solution)/shard_map/ppermute | solution.py:26
  74.5 0.0 copy-done.2
  74.5 0.1 constant_dynamic-slice_fusion.10
  74.6 0.0 collective-permute-done.1
  74.6 14.2 %collective-permute-done.4 = bf16[1,32,3072]{2,1,0:T(8,128)(2,1)S(1)} collective-permute-done((bf16[1,32,3072]{2,1,0:T(8,128)(2,1)S(1)}, bf16[1,32,3072]{2,1,0:T(8,128)(2,1)S(1)}, u32[]{:S(2)}, u32[]{:S(2)}) %collective-permute-start.4) | collective-permute-done | bytes 196640 | tf_op jit(solution)/shard_map/ppermute | solution.py:26
  88.8 7.6 %collective-permute-done.7 = bf16[1,32,3072]{2,1,0:T(8,128)(2,1)S(1)} collective-permute-done((bf16[1,32,3072]{2,1,0:T(8,128)(2,1)S(1)}, bf16[1,32,3072]{2,1,0:T(8,128)(2,1)S(1)}, u32[]{:S(2)}, u32[]{:S(2)}) %collective-permute-start.7) | collective-permute-done | bytes 196640 | tf_op jit(solution)/shard_map/ppermute | solution.py:26
  96.4 1.0 pad_maximum_fusion.2
  97.4 0.0 all-gather.6.cloned.1.call-update
  97.4 0.0 all-gather.8.cloned.1.call-start
  97.5 2.8 collective-permute-start.2
  100.3 11.6 %collective-permute-start.5 = (bf16[1,32,3072]{2,1,0:T(8,128)(2,1)S(1)}, bf16[1,32,3072]{2,1,0:T(8,128)(2,1)S(1)}, u32[]{:S(2)}, u32[]{:S(2)}) collective-permute-start(bf16[1,32,3072]{2,1,0:T(8,128)(2,1)S(1)} %get-tuple-element.22), channel_id=1, source_target_pairs={{0,16},{8,24},{16,0},{24,8},{1,17},{9,25},{17,1},{25,9},{2,18},{10... | collective-permute-start | bytes 589832 | tf_op jit(solution)/shard_map/ppermute | solution.py:26
  111.9 2.5 collective-permute-start.8
  114.5 0.0 collective-permute-done.2
  114.5 12.0 %collective-permute-done.5 = bf16[1,32,3072]{2,1,0:T(8,128)(2,1)S(1)} collective-permute-done((bf16[1,32,3072]{2,1,0:T(8,128)(2,1)S(1)}, bf16[1,32,3072]{2,1,0:T(8,128)(2,1)S(1)}, u32[]{:S(2)}, u32[]{:S(2)}) %collective-permute-start.5) | collective-permute-done | bytes 196640 | tf_op jit(solution)/shard_map/ppermute | solution.py:26
  126.4 7.1 %collective-permute-done.8 = bf16[1,32,3072]{2,1,0:T(8,128)(2,1)S(1)} collective-permute-done((bf16[1,32,3072]{2,1,0:T(8,128)(2,1)S(1)}, bf16[1,32,3072]{2,1,0:T(8,128)(2,1)S(1)}, u32[]{:S(2)}, u32[]{:S(2)}) %collective-permute-start.8) | collective-permute-done | bytes 196640 | tf_op jit(solution)/shard_map/ppermute | solution.py:26
  133.6 0.0 copy-start.3
  133.6 1.0 pad_maximum_fusion
  134.6 0.0 all-gather.8.cloned.1.call-update
  134.6 0.0 copy-done.3
  134.6 0.1 fusion.1
  134.7 0.2 reduce_window_sum.11
  134.9 0.2 select_reduce_fusion
  135.0 0.0 copy-done
  135.1 0.5 convolution_convert_fusion.1
  135.5 0.6 reshape.29
  136.1 78.8 %all_to_all.10 = bf16[64,24,384]{2,1,0:T(8,128)(2,1)S(1)} all-to-all(bf16[64,24,384]{2,1,0:T(8,128)(2,1)S(1)} %reshape.29), channel_id=1, replica_groups=mesh['x'=4,'zlo'=4,'zhi'=4,'y'=4,'core'=2] {'x','zlo','zhi'}, dimensions={0} | all-to-all | bytes 2359296 | tf_op jit(solution)/shard_map/all_to_all | solution.py:53
  215.0 0.6 reshape.30
  215.5 0.0 all-gather.4.cloned.1.call-done
  215.6 5.0 %fusion.4 = f32[192,1024]{1,0:T(8,128)S(1)} fusion(bf16[192,3072]{1,0:T(8,128)(2,1)S(1)} %reshape.30, bf16[1024,3072]{1,0:T(8,128)(2,1)} %bitcast.15), kind=kOutput, calls=%fused_computation.27 | convolution fusion | flops 1207959552 | bytes 8257536 | tf_op jit(solution)/shard_map/dot_general | solution.py:55
  220.6 0.0 all-gather.6.cloned.1.call-done
  220.6 5.1 %fusion = bf16[192,1024]{1,0:T(8,128)(2,1)S(1)} fusion(bf16[192,3072]{1,0:T(8,128)(2,1)S(1)} %reshape.30, bf16[1024,3072]{1,0:T(8,128)(2,1)} %bitcast.16, f32[192,1024]{1,0:T(8,128)S(1)} %fusion.4), kind=kOutput, calls=%fused_computation.4 | convolution fusion | flops 1209139200 | bytes 8650752 | tf_op jit(solution)/shard_map/dot_general | solution.py:58
  225.7 0.0 all-gather.8.cloned.1.call-done
  225.8 4.2 %convolution_convert_fusion = bf16[192,3072]{1,0:T(8,128)(2,1)S(1)} fusion(bf16[192,1024]{1,0:T(8,128)(2,1)S(1)} %fusion, bf16[1024,3072]{1,0:T(8,128)(2,1)} %bitcast.17), kind=kOutput, calls=%fused_computation | convolution fusion | flops 1208549376 | bytes 7864320 | tf_op jit(solution)/shard_map/dot_general | solution.py:63
  230.0 0.6 reshape.34
  230.6 65.6 %all_to_all.11 = bf16[64,24,384]{2,1,0:T(8,128)(2,1)S(1)} all-to-all(bf16[64,24,384]{2,1,0:T(8,128)(2,1)S(1)} %reshape.34), channel_id=1, replica_groups=mesh['x'=4,'zlo'=4,'zhi'=4,'y'=4,'core'=2] {'x','zlo','zhi'}, dimensions={0} | all-to-all | bytes 2359296 | tf_op jit(solution)/shard_map/all_to_all | solution.py:65
  296.2 0.6 reshape.35
  296.8 1.3 convolution_convert_fusion.2
  (1 shorter events, 0.0 us)
Async XLA Ops:
  6.5 128.5 %copy-start = (bf16[128,3072]{1,0:T(8,128)(2,1)S(1)}, bf16[128,3072]{1,0:T(8,128)(2,1)}, u32[]{:S(2)}) copy-start(bf16[128,3072]{1,0:T(8,128)(2,1)} %param.5) | copy-start | bytes 2359300
  6.5 26.0 %copy-start.1 = (bf16[4,32,3072]{2,1,0:T(8,128)(2,1)S(1)}, bf16[4,32,3072]{2,1,0:T(8,128)(2,1)}, u32[]{:S(2)}) copy-start(bf16[4,32,3072]{2,1,0:T(8,128)(2,1)} %param.8) | copy-start | bytes 2359300
  6.5 209.0 %all-gather.4.cloned.1.call-start = ((), (), s32[]{:S(2)}) async-start(), calls=%async_computation.2 | async-start | bytes 7077888 | tf_op jit(solution)/shard_map/all_gather | solution.py:43
  7.9 26.3 %collective-permute-start = (bf16[1,32,3072]{2,1,0:T(8,128)(2,1)S(1)}, bf16[1,32,3072]{2,1,0:T(8,128)(2,1)S(1)}, u32[]{:S(2)}, u32[]{:S(2)}) collective-permute-start(bf16[1,32,3072]{2,1,0:T(8,128)(2,1)S(1)} %get-tuple-element.35), channel_id=1, source_target_pairs={{0,8},{8,16},{16,24},{24,0},{1,9},{9,17},{17,25},{25,1},{2,10},{10... | collective-permute-start | bytes 589832 | tf_op jit(solution)/shard_map/ppermute | solution.py:26
  17.0 26.0 %collective-permute-start.3 = (bf16[1,32,3072]{2,1,0:T(8,128)(2,1)S(1)}, bf16[1,32,3072]{2,1,0:T(8,128)(2,1)S(1)}, u32[]{:S(2)}, u32[]{:S(2)}) collective-permute-start(bf16[1,32,3072]{2,1,0:T(8,128)(2,1)S(1)} %get-tuple-element.34), channel_id=1, source_target_pairs={{0,16},{8,24},{16,0},{24,8},{1,17},{9,25},{17,1},{25,9},{2,18},{10... | collective-permute-start | bytes 589832 | tf_op jit(solution)/shard_map/ppermute | solution.py:26
  27.1 25.3 %collective-permute-start.6 = (bf16[1,32,3072]{2,1,0:T(8,128)(2,1)S(1)}, bf16[1,32,3072]{2,1,0:T(8,128)(2,1)S(1)}, u32[]{:S(2)}, u32[]{:S(2)}) collective-permute-start(bf16[1,32,3072]{2,1,0:T(8,128)(2,1)S(1)} %get-tuple-element.36), channel_id=1, source_target_pairs={{0,24},{8,0},{16,8},{24,16},{1,25},{9,1},{17,9},{25,17},{2,26},{10... | collective-permute-start | bytes 589832 | tf_op jit(solution)/shard_map/ppermute | solution.py:26
  52.4 22.2 %copy-start.2 = (bf16[4,32,3072]{2,1,0:T(8,128)(2,1)S(1)}, bf16[4,32,3072]{2,1,0:T(8,128)(2,1)}, u32[]{:S(2)}) copy-start(bf16[4,32,3072]{2,1,0:T(8,128)(2,1)} %param.9) | copy-start | bytes 2359300
  53.4 167.2 %all-gather.6.cloned.1.call-start = ((), (), s32[]{:S(2)}) async-start(), calls=%async_computation.3 | async-start | bytes 7077888 | tf_op jit(solution)/shard_map/all_gather | solution.py:43
  53.5 21.2 %collective-permute-start.1 = (bf16[1,32,3072]{2,1,0:T(8,128)(2,1)S(1)}, bf16[1,32,3072]{2,1,0:T(8,128)(2,1)S(1)}, u32[]{:S(2)}, u32[]{:S(2)}) collective-permute-start(bf16[1,32,3072]{2,1,0:T(8,128)(2,1)S(1)} %get-tuple-element.19), channel_id=1, source_target_pairs={{0,8},{8,16},{16,24},{24,0},{1,9},{9,17},{17,25},{25,1},{2,10},{10... | collective-permute-start | bytes 589832 | tf_op jit(solution)/shard_map/ppermute | solution.py:26
  56.8 32.0 %collective-permute-start.4 = (bf16[1,32,3072]{2,1,0:T(8,128)(2,1)S(1)}, bf16[1,32,3072]{2,1,0:T(8,128)(2,1)S(1)}, u32[]{:S(2)}, u32[]{:S(2)}) collective-permute-start(bf16[1,32,3072]{2,1,0:T(8,128)(2,1)S(1)} %get-tuple-element.21), channel_id=1, source_target_pairs={{0,16},{8,24},{16,0},{24,8},{1,17},{9,25},{17,1},{25,9},{2,18},{10... | collective-permute-start | bytes 589832 | tf_op jit(solution)/shard_map/ppermute | solution.py:26
  68.1 28.3 %collective-permute-start.7 = (bf16[1,32,3072]{2,1,0:T(8,128)(2,1)S(1)}, bf16[1,32,3072]{2,1,0:T(8,128)(2,1)S(1)}, u32[]{:S(2)}, u32[]{:S(2)}) collective-permute-start(bf16[1,32,3072]{2,1,0:T(8,128)(2,1)S(1)} %get-tuple-element.23), channel_id=1, source_target_pairs={{0,24},{8,0},{16,8},{24,16},{1,25},{9,1},{17,9},{25,17},{2,26},{10... | collective-permute-start | bytes 589832 | tf_op jit(solution)/shard_map/ppermute | solution.py:26
  97.4 128.3 %all-gather.8.cloned.1.call-start = ((), (), s32[]{:S(2)}) async-start(), calls=%async_computation.4 | async-start | bytes 7077888 | tf_op jit(solution)/shard_map/all_gather | solution.py:43
  97.5 17.0 %collective-permute-start.2 = (bf16[1,32,3072]{2,1,0:T(8,128)(2,1)S(1)}, bf16[1,32,3072]{2,1,0:T(8,128)(2,1)S(1)}, u32[]{:S(2)}, u32[]{:S(2)}) collective-permute-start(bf16[1,32,3072]{2,1,0:T(8,128)(2,1)S(1)} %get-tuple-element.20), channel_id=1, source_target_pairs={{0,8},{8,16},{16,24},{24,0},{1,9},{9,17},{17,25},{25,1},{2,10},{10... | collective-permute-start | bytes 589832 | tf_op jit(solution)/shard_map/ppermute | solution.py:26
  100.3 26.2 %collective-permute-start.5 = (bf16[1,32,3072]{2,1,0:T(8,128)(2,1)S(1)}, bf16[1,32,3072]{2,1,0:T(8,128)(2,1)S(1)}, u32[]{:S(2)}, u32[]{:S(2)}) collective-permute-start(bf16[1,32,3072]{2,1,0:T(8,128)(2,1)S(1)} %get-tuple-element.22), channel_id=1, source_target_pairs={{0,16},{8,24},{16,0},{24,8},{1,17},{9,25},{17,1},{25,9},{2,18},{10... | collective-permute-start | bytes 589832 | tf_op jit(solution)/shard_map/ppermute | solution.py:26
  111.9 21.7 %collective-permute-start.8 = (bf16[1,32,3072]{2,1,0:T(8,128)(2,1)S(1)}, bf16[1,32,3072]{2,1,0:T(8,128)(2,1)S(1)}, u32[]{:S(2)}, u32[]{:S(2)}) collective-permute-start(bf16[1,32,3072]{2,1,0:T(8,128)(2,1)S(1)} %get-tuple-element.24), channel_id=1, source_target_pairs={{0,24},{8,0},{16,8},{24,16},{1,25},{9,1},{17,9},{25,17},{2,26},{10... | collective-permute-start | bytes 589832 | tf_op jit(solution)/shard_map/ppermute | solution.py:26
  133.6 1.0 copy-start.3
Sparse Core Ops, SparseCore 0:
  53.5 56.2 all-gather.3
  111.9 48.7 all-gather.5
  162.8 48.7 all-gather.7

commit v3 on v1

v3 whole, which is shorter than its diff:
```python
import jax
import jax.numpy as jnp
from jax import lax
from jax.experimental import pallas as pl
from jax.experimental.pallas import tpu as pltpu
from jax.sharding import Mesh, PartitionSpec as P

CAP = 3
CHUNKS = 8
PARTS = 2
MIB = 1 << 20


def swiglu_kernel(x_ref, *refs):
    weights, (out_ref, held, total, arrival) = refs[:-4], refs[-4:]
    blocks, triple, width = weights[0].shape
    rows = triple // 3
    copies = [
        pltpu.make_async_copy(weight, held.at[i], arrival.at[i]) for i, weight in enumerate(weights)
    ]
    for copy in copies:
        copy.start()
    across = (((1,), (1,)), ((), ()))
    for i, copy in enumerate(copies):
        copy.wait()

        def matrix(which):
            return held[i, :, which * rows : (which + 1) * rows, :].reshape(blocks * rows, width)

        gate = lax.dot_general(x_ref[...], matrix(0), across, preferred_element_type=jnp.float32)
        up = lax.dot_general(x_ref[...], matrix(1), across, preferred_element_type=jnp.float32)
        hidden = (gate / (1.0 + jnp.exp(-gate)) * up).astype(jnp.bfloat16)
        product = jnp.dot(hidden, matrix(2), preferred_element_type=jnp.float32)
        if i == 0:
            total[...] = product
        elif i < len(copies) - 1:
            total[...] += product
        else:
            out_ref[...] = (total[...] + product).astype(out_ref.dtype)


def swiglu(x, weights):
    slots, width = x.shape
    blocks, triple, _ = weights[0].shape
    units = len(weights) * blocks * triple // 3
    return pl.pallas_call(
        swiglu_kernel,
        out_shape=jax.ShapeDtypeStruct(x.shape, jnp.bfloat16),
        in_specs=[pl.BlockSpec(memory_space=pltpu.VMEM)]
        + [pl.BlockSpec(memory_space=pl.ANY)] * len(weights),
        out_specs=pl.BlockSpec(memory_space=pltpu.VMEM),
        scratch_shapes=[
            pltpu.VMEM((len(weights), blocks, triple, width), jnp.bfloat16),
            pltpu.VMEM((slots, width), jnp.float32),
            pltpu.SemaphoreType.DMA((len(weights),)),
        ],
        compiler_params=pltpu.CompilerParams(vmem_limit_bytes=48 * MIB),
        cost_estimate=pl.CostEstimate(
            flops=6 * slots * units * width,
            bytes_accessed=6 * units * width + 4 * slots * width,
            transcendentals=slots * units,
        ),
    )(x, *weights)


def shards(tokens, expert_ids, gate_weight, up_weight, down_weight):
    exp_dev, unit_rows, width = gate_weight.shape
    routes = ("x", "zlo", "zhi")
    experts = exp_dev * lax.axis_size("x") * lax.axis_size("zlo")
    chunk = width // CHUNKS
    slots = experts * CAP
    ring = lax.axis_size("zhi")
    place = lax.axis_index("zhi")
    part_rows = unit_rows // PARTS

    def tied(*values):
        return lax.optimization_barrier(values)

    def shifted(value, axis, step):
        size = lax.axis_size(axis)
        return lax.ppermute(value, axis, [(i, (i + step) % size) for i in range(size)])

    def outgoing(step, part):
        target = lax.rem(place + step, ring)
        return jnp.concatenate(
            [
                lax.dynamic_slice(w, (target, part * part_rows, 0), (1, part_rows, width))
                for w in (gate_weight, up_weight, down_weight)
            ],
            axis=1,
        )

    def over_z(pieces):
        order = sorted(range(1, ring), key=lambda step: abs(2 * step - ring))
        return [shifted(pieces[step], "zhi", step) for step in order] + [pieces[0]]

    def over_plane(part):
        return lax.all_gather(part, ("y", "core"), axis=0, tiled=True)

    def joined(pieces):
        return jnp.concatenate(pieces, axis=0)

    early = tied(*[outgoing(step, 0) for step in range(ring)])
    late = tied(*[outgoing(step, 1) for step in range(ring)])
    first = joined(tied(*over_z(list(early))))
    first, *late = tied(first, *late)
    second = joined(tied(*over_z(late)))
    tokens, second = tied(tokens, second)
    first, second = over_plane(first), over_plane(second)

    flat_ids = expert_ids[:, 0]
    matches = (flat_ids[:, None] == jnp.arange(experts, dtype=jnp.int32)[None, :]).astype(jnp.int32)
    rank_of = jnp.sum((jnp.cumsum(matches, axis=0) - 1) * matches, axis=1)
    position = flat_ids * CAP + rank_of
    selector = (position[None, :] == jnp.arange(slots, dtype=jnp.int32)[:, None]).astype(jnp.bfloat16)
    packed = jnp.dot(selector, tokens, preferred_element_type=jnp.float32).astype(jnp.bfloat16)
    packed = packed.reshape(experts, CAP * CHUNKS, chunk)
    arrived = lax.all_to_all(packed, routes, split_axis=0, concat_axis=0, tiled=True)

    result = swiglu(arrived.reshape(slots, width), [first, second])
    result = result.reshape(experts, CAP * CHUNKS, chunk)
    returned = lax.all_to_all(result, routes, split_axis=0, concat_axis=0, tiled=True)
    returned = returned.reshape(slots, width)
    output = lax.dot_general(
        selector, returned, (((0,), (0,)), ((), ())), preferred_element_type=jnp.float32
    )
    return output.astype(jnp.bfloat16)


def solution(mesh):
    fine = Mesh(mesh.devices.reshape(4, 4, 4, 4, 2), ("x", "zlo", "zhi", "y", "core"))
    everyone = ("x", "zlo", "zhi", "y", "core")
    group = ("x", "zlo")
    sub = ("zhi", "y", "core")
    return jax.shard_map(
        shards,
        mesh=fine,
        in_specs=(
            P(everyone, None),
            P(everyone, None),
            P(group, sub, None),
            P(group, sub, None),
            P(group, sub, None),
        ),
        out_specs=P(everyone, None),
        check_vma=False,
    )
```

time: 306 us -> 295 us (0.964)
  the two profiles are of different devices: /device:TPU:56 before, /device:TPU:32 now
where the time goes in v3:
time: 295 us; the launch traced here: 294 us
  blocking collectives  139 us (47%)
  waiting for transfers between devices  76.5 us (26%)
  starting transfers between devices  46.4 us (16%)
  between operations  13.7 us (5%)
  Pallas kernels  9.54 us (3%)
  local copies, waits for them, and re-layouts  4.81 us (2%)
  other arithmetic  2.95 us (1%)
    ppermute x6, waiting for transfers between devices, shifted(): lax.ppermute(value, axis, [(i, (i + step) % size) for i in range(size)])  76.5 us
    all_to_all x1, blocking collectives, shards(): lax.all_to_all(packed, routes, split_axis=0, concat_axis=0, tiled=True)  72.2 us
    all_to_all x1, blocking collectives, shards(): lax.all_to_all(result, routes, split_axis=0, concat_axis=0, tiled=True)  66.5 us
    ppermute x6, starting transfers between devices, shifted(): lax.ppermute(value, axis, [(i, (i + step) % size) for i in range(size)])  46.3 us
    pallas_call x1, Pallas kernels, swiglu(): pl.pallas_call(swiglu_kernel, out_shape=jax.ShapeDtypeStruct(x.shape, jnp...  9.54 us
  transfers between devices with their start and end apart: 8, of which 3 were waited for; matrix products, arithmetic and copies ran while one was open for 1% of the time, Pallas kernels for 0%

profile of v3, /device:TPU:32, one launch (start us, length us, event | category | flops | bytes accessed | tf_op | source)
XLA Modules:
  0.0 294.4 jit_solution(3247280067638719306)
XLA Ops:
  6.5 0.0 copy-start
  6.5 0.0 copy-start.2
  6.5 0.0 copy-start.1
  6.5 0.0 all-gather.3.cloned.1.call-start
  6.6 1.4 constant_dynamic-slice_fusion.23
  8.0 0.1 copy-done.2
  8.1 0.2 copy-done.1
  8.3 0.1 constant_dynamic-slice_fusion
  8.6 14.8 %collective-permute-start = (bf16[1,48,3072]{2,1,0:T(8,128)(2,1)S(1)}, bf16[1,48,3072]{2,1,0:T(8,128)(2,1)S(1)}, u32[]{:S(2)}, u32[]{:S(2)}) collective-permute-start(bf16[1,48,3072]{2,1,0:T(8,128)(2,1)S(1)} %pad_maximum_fusion.4), channel_id=1, source_target_pairs={{0,16},{8,24},{16,0},{24,8},{1,17},{9,25},{17,1},{25,9},{2,18},{10... | collective-permute-start | bytes 884744 | tf_op jit(solution)/shard_map/ppermute | solution.py:81
  23.4 4.3 %collective-permute-start.1 = (bf16[1,48,3072]{2,1,0:T(8,128)(2,1)S(1)}, bf16[1,48,3072]{2,1,0:T(8,128)(2,1)S(1)}, u32[]{:S(2)}, u32[]{:S(2)}) collective-permute-start(bf16[1,48,3072]{2,1,0:T(8,128)(2,1)S(1)} %pad_maximum_fusion.3), channel_id=1, source_target_pairs={{0,8},{8,16},{16,24},{24,0},{1,9},{9,17},{17,25},{25,1},{2,10},{10... | collective-permute-start | bytes 884744 | tf_op jit(solution)/shard_map/ppermute | solution.py:81
  27.7 5.5 %collective-permute-start.2 = (bf16[1,48,3072]{2,1,0:T(8,128)(2,1)S(1)}, bf16[1,48,3072]{2,1,0:T(8,128)(2,1)S(1)}, u32[]{:S(2)}, u32[]{:S(2)}) collective-permute-start(bf16[1,48,3072]{2,1,0:T(8,128)(2,1)S(1)} %pad_maximum_fusion.5), channel_id=1, source_target_pairs={{0,24},{8,0},{16,8},{24,16},{1,25},{9,1},{17,9},{25,17},{2,26},{10... | collective-permute-start | bytes 884744 | tf_op jit(solution)/shard_map/ppermute | solution.py:81
  33.3 26.0 %collective-permute-done = bf16[1,48,3072]{2,1,0:T(8,128)(2,1)S(1)} collective-permute-done((bf16[1,48,3072]{2,1,0:T(8,128)(2,1)S(1)}, bf16[1,48,3072]{2,1,0:T(8,128)(2,1)S(1)}, u32[]{:S(2)}, u32[]{:S(2)}) %collective-permute-start) | collective-permute-done | bytes 294944 | tf_op jit(solution)/shard_map/ppermute | solution.py:81
  59.2 0.0 collective-permute-done.1
  59.3 9.3 %collective-permute-done.2 = bf16[1,48,3072]{2,1,0:T(8,128)(2,1)S(1)} collective-permute-done((bf16[1,48,3072]{2,1,0:T(8,128)(2,1)S(1)}, bf16[1,48,3072]{2,1,0:T(8,128)(2,1)S(1)}, u32[]{:S(2)}, u32[]{:S(2)}) %collective-permute-start.2) | collective-permute-done | bytes 294944 | tf_op jit(solution)/shard_map/ppermute | solution.py:81
  68.6 1.2 pad_maximum_fusion
  69.8 0.0 all-gather.3.cloned.1.call-update
  69.8 0.0 all-gather.5.cloned.1.call-start
  69.8 6.6 %collective-permute-start.3 = (bf16[1,48,3072]{2,1,0:T(8,128)(2,1)S(1)}, bf16[1,48,3072]{2,1,0:T(8,128)(2,1)S(1)}, u32[]{:S(2)}, u32[]{:S(2)}) collective-permute-start(bf16[1,48,3072]{2,1,0:T(8,128)(2,1)S(1)} %pad_maximum_fusion.8), channel_id=1, source_target_pairs={{0,16},{8,24},{16,0},{24,8},{1,17},{9,25},{17,1},{25,9},{2,18},{10... | collective-permute-start | bytes 884744 | tf_op jit(solution)/shard_map/ppermute | solution.py:81
  76.5 8.0 %collective-permute-start.4 = (bf16[1,48,3072]{2,1,0:T(8,128)(2,1)S(1)}, bf16[1,48,3072]{2,1,0:T(8,128)(2,1)S(1)}, u32[]{:S(2)}, u32[]{:S(2)}) collective-permute-start(bf16[1,48,3072]{2,1,0:T(8,128)(2,1)S(1)} %pad_maximum_fusion.7), channel_id=1, source_target_pairs={{0,8},{8,16},{16,24},{24,0},{1,9},{9,17},{17,25},{25,1},{2,10},{10... | collective-permute-start | bytes 884744 | tf_op jit(solution)/shard_map/ppermute | solution.py:81
  84.4 7.2 %collective-permute-start.5 = (bf16[1,48,3072]{2,1,0:T(8,128)(2,1)S(1)}, bf16[1,48,3072]{2,1,0:T(8,128)(2,1)S(1)}, u32[]{:S(2)}, u32[]{:S(2)}) collective-permute-start(bf16[1,48,3072]{2,1,0:T(8,128)(2,1)S(1)} %pad_maximum_fusion.9), channel_id=1, source_target_pairs={{0,24},{8,0},{16,8},{24,16},{1,25},{9,1},{17,9},{25,17},{2,26},{10... | collective-permute-start | bytes 884744 | tf_op jit(solution)/shard_map/ppermute | solution.py:81
  91.6 0.0 collective-permute-done.3
  91.6 41.2 %collective-permute-done.4 = bf16[1,48,3072]{2,1,0:T(8,128)(2,1)S(1)} collective-permute-done((bf16[1,48,3072]{2,1,0:T(8,128)(2,1)S(1)}, bf16[1,48,3072]{2,1,0:T(8,128)(2,1)S(1)}, u32[]{:S(2)}, u32[]{:S(2)}) %collective-permute-start.4) | collective-permute-done | bytes 294944 | tf_op jit(solution)/shard_map/ppermute | solution.py:81
  132.8 0.0 collective-permute-done.5
  132.8 1.2 pad_maximum_fusion.1
  134.0 0.0 copy-start.3
  134.0 0.0 all-gather.5.cloned.1.call-update
  134.0 0.6 copy-done.3
  134.6 0.1 fusion
  134.7 0.2 reduce_window_sum.11
  134.9 0.2 select_reduce_fusion
  135.1 0.0 copy-done
  135.1 0.5 convolution_convert_fusion
  135.6 0.6 reshape.20
  136.2 72.2 %all_to_all.10 = bf16[64,24,384]{2,1,0:T(8,128)(2,1)S(1)} all-to-all(bf16[64,24,384]{2,1,0:T(8,128)(2,1)S(1)} %reshape.20), channel_id=1, replica_groups=mesh['x'=4,'zlo'=4,'zhi'=4,'y'=4,'core'=2] {'x','zlo','zhi'}, dimensions={0} | all-to-all | bytes 2359296 | tf_op jit(solution)/shard_map/all_to_all | solution.py:118
  208.4 0.6 reshape.21.x_ref
  209.0 0.0 all-gather.3.cloned.1.call-done.refs_0_
  209.0 0.0 all-gather.5.cloned.1.call-done.refs_1_
  209.0 9.5 %shard_map.55 = bf16[192,3072]{1,0:T(8,128)(2,1)S(1)} custom-call(bf16[192,3072]{1,0:T(8,128)(2,1)S(1)} %reshape.21.x_ref, bf16[32,48,3072]{2,1,0:T(8,128)(2,1)} %all-gather.3.cloned.1.call-done.refs_0_, bf16[32,48,3072]{2,1,0:T(8,128)(2,1)} %all-gather.5.cloned.1.call-done.refs_1_), custom_call_target="tpu_custom_call" | custom-call | flops 3623878656 | bytes 21233664 | tf_op jit(solution)/shard_map/pallas_call | solution.py:46
  218.6 0.6 reshape.22
  219.2 66.5 %all_to_all.11 = bf16[64,24,384]{2,1,0:T(8,128)(2,1)S(1)} all-to-all(bf16[64,24,384]{2,1,0:T(8,128)(2,1)S(1)} %reshape.22), channel_id=1, replica_groups=mesh['x'=4,'zlo'=4,'zhi'=4,'y'=4,'core'=2] {'x','zlo','zhi'}, dimensions={0} | all-to-all | bytes 2359296 | tf_op jit(solution)/shard_map/all_to_all | solution.py:122
  285.7 0.6 reshape.23
  286.3 1.3 convolution_convert_fusion.1
  (9 shorter events, 0.2 us)
Async XLA Ops:
  6.5 128.6 %copy-start = (bf16[128,3072]{1,0:T(8,128)(2,1)S(1)}, bf16[128,3072]{1,0:T(8,128)(2,1)}, u32[]{:S(2)}) copy-start(bf16[128,3072]{1,0:T(8,128)(2,1)} %param.5) | copy-start | bytes 2359300
  6.5 1.5 copy-start.2
  6.5 1.8 copy-start.1
  6.5 202.5 %all-gather.3.cloned.1.call-start = ((), (), s32[]{:S(2)}) async-start(), calls=%async_computation.2 | async-start | bytes 10616832 | tf_op jit(solution)/shard_map/all_gather | solution.py:98
  8.6 50.7 %collective-permute-start = (bf16[1,48,3072]{2,1,0:T(8,128)(2,1)S(1)}, bf16[1,48,3072]{2,1,0:T(8,128)(2,1)S(1)}, u32[]{:S(2)}, u32[]{:S(2)}) collective-permute-start(bf16[1,48,3072]{2,1,0:T(8,128)(2,1)S(1)} %pad_maximum_fusion.4), channel_id=1, source_target_pairs={{0,16},{8,24},{16,0},{24,8},{1,17},{9,25},{17,1},{25,9},{2,18},{10... | collective-permute-start | bytes 884744 | tf_op jit(solution)/shard_map/ppermute | solution.py:81
  23.4 35.9 %collective-permute-start.1 = (bf16[1,48,3072]{2,1,0:T(8,128)(2,1)S(1)}, bf16[1,48,3072]{2,1,0:T(8,128)(2,1)S(1)}, u32[]{:S(2)}, u32[]{:S(2)}) collective-permute-start(bf16[1,48,3072]{2,1,0:T(8,128)(2,1)S(1)} %pad_maximum_fusion.3), channel_id=1, source_target_pairs={{0,8},{8,16},{16,24},{24,0},{1,9},{9,17},{17,25},{25,1},{2,10},{10... | collective-permute-start | bytes 884744 | tf_op jit(solution)/shard_map/ppermute | solution.py:81
  27.7 40.9 %collective-permute-start.2 = (bf16[1,48,3072]{2,1,0:T(8,128)(2,1)S(1)}, bf16[1,48,3072]{2,1,0:T(8,128)(2,1)S(1)}, u32[]{:S(2)}, u32[]{:S(2)}) collective-permute-start(bf16[1,48,3072]{2,1,0:T(8,128)(2,1)S(1)} %pad_maximum_fusion.5), channel_id=1, source_target_pairs={{0,24},{8,0},{16,8},{24,16},{1,25},{9,1},{17,9},{25,17},{2,26},{10... | collective-permute-start | bytes 884744 | tf_op jit(solution)/shard_map/ppermute | solution.py:81
  69.8 139.2 %all-gather.5.cloned.1.call-start = ((), (), s32[]{:S(2)}) async-start(), calls=%async_computation.3 | async-start | bytes 10616832 | tf_op jit(solution)/shard_map/all_gather | solution.py:98
  69.8 21.8 %collective-permute-start.3 = (bf16[1,48,3072]{2,1,0:T(8,128)(2,1)S(1)}, bf16[1,48,3072]{2,1,0:T(8,128)(2,1)S(1)}, u32[]{:S(2)}, u32[]{:S(2)}) collective-permute-start(bf16[1,48,3072]{2,1,0:T(8,128)(2,1)S(1)} %pad_maximum_fusion.8), channel_id=1, source_target_pairs={{0,16},{8,24},{16,0},{24,8},{1,17},{9,25},{17,1},{25,9},{2,18},{10... | collective-permute-start | bytes 884744 | tf_op jit(solution)/shard_map/ppermute | solution.py:81
  76.5 56.3 %collective-permute-start.4 = (bf16[1,48,3072]{2,1,0:T(8,128)(2,1)S(1)}, bf16[1,48,3072]{2,1,0:T(8,128)(2,1)S(1)}, u32[]{:S(2)}, u32[]{:S(2)}) collective-permute-start(bf16[1,48,3072]{2,1,0:T(8,128)(2,1)S(1)} %pad_maximum_fusion.7), channel_id=1, source_target_pairs={{0,8},{8,16},{16,24},{24,0},{1,9},{9,17},{17,25},{25,1},{2,10},{10... | collective-permute-start | bytes 884744 | tf_op jit(solution)/shard_map/ppermute | solution.py:81
  84.4 48.4 %collective-permute-start.5 = (bf16[1,48,3072]{2,1,0:T(8,128)(2,1)S(1)}, bf16[1,48,3072]{2,1,0:T(8,128)(2,1)S(1)}, u32[]{:S(2)}, u32[]{:S(2)}) collective-permute-start(bf16[1,48,3072]{2,1,0:T(8,128)(2,1)S(1)} %pad_maximum_fusion.9), channel_id=1, source_target_pairs={{0,24},{8,0},{16,8},{24,16},{1,25},{9,1},{17,9},{25,17},{2,26},{10... | collective-permute-start | bytes 884744 | tf_op jit(solution)/shard_map/ppermute | solution.py:81
  134.0 0.7 copy-start.3
Sparse Core Ops, SparseCore 0:
  69.9 65.7 all-gather.2
  137.8 62.0 all-gather.4

commit v4 on v3

--- a/solution.py
+++ b/solution.py
@@ -8,21 +8,29 @@
 CAP = 3
 CHUNKS = 8
 PARTS = 2
+PIECES = 4
+AHEAD = 2
 MIB = 1 << 20
 
 
 def swiglu_kernel(x_ref, *refs):
     weights, (out_ref, held, total, arrival) = refs[:-4], refs[-4:]
-    blocks, triple, width = weights[0].shape
+    pieces, blocks, triple, width = held.shape
     rows = triple // 3
+    each = pieces // len(weights)
     copies = [
-        pltpu.make_async_copy(weight, held.at[i], arrival.at[i]) for i, weight in enumerate(weights)
+        pltpu.make_async_copy(
+            weights[i // each].at[pl.ds(i % each * blocks, blocks)], held.at[i], arrival.at[i]
+        )
+        for i in range(pieces)
     ]
-    for copy in copies:
+    for copy in copies[:AHEAD]:
         copy.start()
     across = (((1,), (1,)), ((), ()))
     for i, copy in enumerate(copies):
         copy.wait()
+        for later in copies[i + AHEAD : i + AHEAD + 1]:
+            later.start()
 
         def matrix(which):
             return held[i, :, which * rows : (which + 1) * rows, :].reshape(blocks * rows, width)
@@ -50,9 +58,9 @@
         + [pl.BlockSpec(memory_space=pl.ANY)] * len(weights),
         out_specs=pl.BlockSpec(memory_space=pltpu.VMEM),
         scratch_shapes=[
-            pltpu.VMEM((len(weights), blocks, triple, width), jnp.bfloat16),
+            pltpu.VMEM((PIECES, len(weights) * blocks // PIECES, triple, width), jnp.bfloat16),
             pltpu.VMEM((slots, width), jnp.float32),
-            pltpu.SemaphoreType.DMA((len(weights),)),
+            pltpu.SemaphoreType.DMA((PIECES,)),
         ],
         compiler_params=pltpu.CompilerParams(vmem_limit_bytes=48 * MIB),
         cost_estimate=pl.CostEstimate(

time: 295 us -> 294 us (level)
  no operation moved by 1% of the time
where the time goes in v4:
time: 294 us; the launch traced here: 293 us
  blocking collectives  139 us (47%)
  waiting for transfers between devices  76.5 us (26%)
  starting transfers between devices  46.4 us (16%)
  between operations  13.7 us (5%)
  Pallas kernels  8.61 us (3%)
  local copies, waits for them, and re-layouts  4.81 us (2%)
  other arithmetic  2.95 us (1%)
    ppermute x6, waiting for transfers between devices, shifted(): lax.ppermute(value, axis, [(i, (i + step) % size) for i in range(size)])  76.5 us
    all_to_all x1, blocking collectives, shards(): lax.all_to_all(packed, routes, split_axis=0, concat_axis=0, tiled=True)  72.2 us
    all_to_all x1, blocking collectives, shards(): lax.all_to_all(result, routes, split_axis=0, concat_axis=0, tiled=True)  66.5 us
    ppermute x6, starting transfers between devices, shifted(): lax.ppermute(value, axis, [(i, (i + step) % size) for i in range(size)])  46.3 us
    pallas_call x1, Pallas kernels, swiglu(): pl.pallas_call(swiglu_kernel, out_shape=jax.ShapeDtypeStruct(x.shape, jnp...  8.61 us
  transfers between devices with their start and end apart: 8, of which 3 were waited for; matrix products, arithmetic and copies ran while one was open for 1% of the time, Pallas kernels for 0%

profile of v4, /device:TPU:32, one launch (start us, length us, event | category | flops | bytes accessed | tf_op | source)
XLA Modules:
  0.0 293.5 jit_solution(13029290165599321334)
XLA Ops:
  6.5 0.0 copy-start
  6.5 0.0 copy-start.2
  6.5 0.0 copy-start.1
  6.5 0.0 all-gather.3.cloned.1.call-start
  6.6 1.4 constant_dynamic-slice_fusion.23
  8.0 0.1 copy-done.2
  8.1 0.2 copy-done.1
  8.3 0.1 constant_dynamic-slice_fusion
  8.6 14.8 %collective-permute-start = (bf16[1,48,3072]{2,1,0:T(8,128)(2,1)S(1)}, bf16[1,48,3072]{2,1,0:T(8,128)(2,1)S(1)}, u32[]{:S(2)}, u32[]{:S(2)}) collective-permute-start(bf16[1,48,3072]{2,1,0:T(8,128)(2,1)S(1)} %pad_maximum_fusion.4), channel_id=1, source_target_pairs={{0,16},{8,24},{16,0},{24,8},{1,17},{9,25},{17,1},{25,9},{2,18},{10... | collective-permute-start | bytes 884744 | tf_op jit(solution)/shard_map/ppermute | solution.py:89
  23.4 4.3 %collective-permute-start.1 = (bf16[1,48,3072]{2,1,0:T(8,128)(2,1)S(1)}, bf16[1,48,3072]{2,1,0:T(8,128)(2,1)S(1)}, u32[]{:S(2)}, u32[]{:S(2)}) collective-permute-start(bf16[1,48,3072]{2,1,0:T(8,128)(2,1)S(1)} %pad_maximum_fusion.3), channel_id=1, source_target_pairs={{0,8},{8,16},{16,24},{24,0},{1,9},{9,17},{17,25},{25,1},{2,10},{10... | collective-permute-start | bytes 884744 | tf_op jit(solution)/shard_map/ppermute | solution.py:89
  27.7 5.5 %collective-permute-start.2 = (bf16[1,48,3072]{2,1,0:T(8,128)(2,1)S(1)}, bf16[1,48,3072]{2,1,0:T(8,128)(2,1)S(1)}, u32[]{:S(2)}, u32[]{:S(2)}) collective-permute-start(bf16[1,48,3072]{2,1,0:T(8,128)(2,1)S(1)} %pad_maximum_fusion.5), channel_id=1, source_target_pairs={{0,24},{8,0},{16,8},{24,16},{1,25},{9,1},{17,9},{25,17},{2,26},{10... | collective-permute-start | bytes 884744 | tf_op jit(solution)/shard_map/ppermute | solution.py:89
  33.3 26.0 %collective-permute-done = bf16[1,48,3072]{2,1,0:T(8,128)(2,1)S(1)} collective-permute-done((bf16[1,48,3072]{2,1,0:T(8,128)(2,1)S(1)}, bf16[1,48,3072]{2,1,0:T(8,128)(2,1)S(1)}, u32[]{:S(2)}, u32[]{:S(2)}) %collective-permute-start) | collective-permute-done | bytes 294944 | tf_op jit(solution)/shard_map/ppermute | solution.py:89
  59.2 0.0 collective-permute-done.1
  59.3 9.3 %collective-permute-done.2 = bf16[1,48,3072]{2,1,0:T(8,128)(2,1)S(1)} collective-permute-done((bf16[1,48,3072]{2,1,0:T(8,128)(2,1)S(1)}, bf16[1,48,3072]{2,1,0:T(8,128)(2,1)S(1)}, u32[]{:S(2)}, u32[]{:S(2)}) %collective-permute-start.2) | collective-permute-done | bytes 294944 | tf_op jit(solution)/shard_map/ppermute | solution.py:89
  68.6 1.2 pad_maximum_fusion
  69.8 0.0 all-gather.3.cloned.1.call-update
  69.8 0.0 all-gather.5.cloned.1.call-start
  69.8 6.6 %collective-permute-start.3 = (bf16[1,48,3072]{2,1,0:T(8,128)(2,1)S(1)}, bf16[1,48,3072]{2,1,0:T(8,128)(2,1)S(1)}, u32[]{:S(2)}, u32[]{:S(2)}) collective-permute-start(bf16[1,48,3072]{2,1,0:T(8,128)(2,1)S(1)} %pad_maximum_fusion.8), channel_id=1, source_target_pairs={{0,16},{8,24},{16,0},{24,8},{1,17},{9,25},{17,1},{25,9},{2,18},{10... | collective-permute-start | bytes 884744 | tf_op jit(solution)/shard_map/ppermute | solution.py:89
  76.5 8.0 %collective-permute-start.4 = (bf16[1,48,3072]{2,1,0:T(8,128)(2,1)S(1)}, bf16[1,48,3072]{2,1,0:T(8,128)(2,1)S(1)}, u32[]{:S(2)}, u32[]{:S(2)}) collective-permute-start(bf16[1,48,3072]{2,1,0:T(8,128)(2,1)S(1)} %pad_maximum_fusion.7), channel_id=1, source_target_pairs={{0,8},{8,16},{16,24},{24,0},{1,9},{9,17},{17,25},{25,1},{2,10},{10... | collective-permute-start | bytes 884744 | tf_op jit(solution)/shard_map/ppermute | solution.py:89
  84.4 7.2 %collective-permute-start.5 = (bf16[1,48,3072]{2,1,0:T(8,128)(2,1)S(1)}, bf16[1,48,3072]{2,1,0:T(8,128)(2,1)S(1)}, u32[]{:S(2)}, u32[]{:S(2)}) collective-permute-start(bf16[1,48,3072]{2,1,0:T(8,128)(2,1)S(1)} %pad_maximum_fusion.9), channel_id=1, source_target_pairs={{0,24},{8,0},{16,8},{24,16},{1,25},{9,1},{17,9},{25,17},{2,26},{10... | collective-permute-start | bytes 884744 | tf_op jit(solution)/shard_map/ppermute | solution.py:89
  91.6 0.0 collective-permute-done.3
  91.6 41.2 %collective-permute-done.4 = bf16[1,48,3072]{2,1,0:T(8,128)(2,1)S(1)} collective-permute-done((bf16[1,48,3072]{2,1,0:T(8,128)(2,1)S(1)}, bf16[1,48,3072]{2,1,0:T(8,128)(2,1)S(1)}, u32[]{:S(2)}, u32[]{:S(2)}) %collective-permute-start.4) | collective-permute-done | bytes 294944 | tf_op jit(solution)/shard_map/ppermute | solution.py:89
  132.8 0.0 collective-permute-done.5
  132.8 1.2 pad_maximum_fusion.1
  134.0 0.0 copy-start.3
  134.0 0.0 all-gather.5.cloned.1.call-update
  134.0 0.6 copy-done.3
  134.6 0.1 fusion
  134.7 0.2 reduce_window_sum.11
  134.9 0.2 select_reduce_fusion
  135.1 0.0 copy-done
  135.1 0.5 convolution_convert_fusion
  135.6 0.6 reshape.20
  136.2 72.2 %all_to_all.10 = bf16[64,24,384]{2,1,0:T(8,128)(2,1)S(1)} all-to-all(bf16[64,24,384]{2,1,0:T(8,128)(2,1)S(1)} %reshape.20), channel_id=1, replica_groups=mesh['x'=4,'zlo'=4,'zhi'=4,'y'=4,'core'=2] {'x','zlo','zhi'}, dimensions={0} | all-to-all | bytes 2359296 | tf_op jit(solution)/shard_map/all_to_all | solution.py:126
  208.4 0.6 reshape.21.x_ref
  209.0 0.0 all-gather.3.cloned.1.call-done.refs_0_
  209.0 0.0 all-gather.5.cloned.1.call-done.refs_1_
  209.0 8.6 %shard_map.55 = bf16[192,3072]{1,0:T(8,128)(2,1)S(1)} custom-call(bf16[192,3072]{1,0:T(8,128)(2,1)S(1)} %reshape.21.x_ref, bf16[32,48,3072]{2,1,0:T(8,128)(2,1)} %all-gather.3.cloned.1.call-done.refs_0_, bf16[32,48,3072]{2,1,0:T(8,128)(2,1)} %all-gather.5.cloned.1.call-done.refs_1_), custom_call_target="tpu_custom_call" | custom-call | flops 3623878656 | bytes 21233664 | tf_op jit(solution)/shard_map/pallas_call | solution.py:54
  217.7 0.6 reshape.22
  218.3 66.5 %all_to_all.11 = bf16[64,24,384]{2,1,0:T(8,128)(2,1)S(1)} all-to-all(bf16[64,24,384]{2,1,0:T(8,128)(2,1)S(1)} %reshape.22), channel_id=1, replica_groups=mesh['x'=4,'zlo'=4,'zhi'=4,'y'=4,'core'=2] {'x','zlo','zhi'}, dimensions={0} | all-to-all | bytes 2359296 | tf_op jit(solution)/shard_map/all_to_all | solution.py:130
  284.8 0.6 reshape.23
  285.4 1.3 convolution_convert_fusion.1
  (9 shorter events, 0.2 us)
Async XLA Ops:
  6.5 128.6 %copy-start = (bf16[128,3072]{1,0:T(8,128)(2,1)S(1)}, bf16[128,3072]{1,0:T(8,128)(2,1)}, u32[]{:S(2)}) copy-start(bf16[128,3072]{1,0:T(8,128)(2,1)} %param.5) | copy-start | bytes 2359300
  6.5 1.5 copy-start.2
  6.5 1.8 copy-start.1
  6.5 202.5 %all-gather.3.cloned.1.call-start = ((), (), s32[]{:S(2)}) async-start(), calls=%async_computation.2 | async-start | bytes 10616832 | tf_op jit(solution)/shard_map/all_gather | solution.py:106
  8.6 50.7 %collective-permute-start = (bf16[1,48,3072]{2,1,0:T(8,128)(2,1)S(1)}, bf16[1,48,3072]{2,1,0:T(8,128)(2,1)S(1)}, u32[]{:S(2)}, u32[]{:S(2)}) collective-permute-start(bf16[1,48,3072]{2,1,0:T(8,128)(2,1)S(1)} %pad_maximum_fusion.4), channel_id=1, source_target_pairs={{0,16},{8,24},{16,0},{24,8},{1,17},{9,25},{17,1},{25,9},{2,18},{10... | collective-permute-start | bytes 884744 | tf_op jit(solution)/shard_map/ppermute | solution.py:89
  23.4 35.9 %collective-permute-start.1 = (bf16[1,48,3072]{2,1,0:T(8,128)(2,1)S(1)}, bf16[1,48,3072]{2,1,0:T(8,128)(2,1)S(1)}, u32[]{:S(2)}, u32[]{:S(2)}) collective-permute-start(bf16[1,48,3072]{2,1,0:T(8,128)(2,1)S(1)} %pad_maximum_fusion.3), channel_id=1, source_target_pairs={{0,8},{8,16},{16,24},{24,0},{1,9},{9,17},{17,25},{25,1},{2,10},{10... | collective-permute-start | bytes 884744 | tf_op jit(solution)/shard_map/ppermute | solution.py:89
  27.7 40.9 %collective-permute-start.2 = (bf16[1,48,3072]{2,1,0:T(8,128)(2,1)S(1)}, bf16[1,48,3072]{2,1,0:T(8,128)(2,1)S(1)}, u32[]{:S(2)}, u32[]{:S(2)}) collective-permute-start(bf16[1,48,3072]{2,1,0:T(8,128)(2,1)S(1)} %pad_maximum_fusion.5), channel_id=1, source_target_pairs={{0,24},{8,0},{16,8},{24,16},{1,25},{9,1},{17,9},{25,17},{2,26},{10... | collective-permute-start | bytes 884744 | tf_op jit(solution)/shard_map/ppermute | solution.py:89
  69.8 139.2 %all-gather.5.cloned.1.call-start = ((), (), s32[]{:S(2)}) async-start(), calls=%async_computation.3 | async-start | bytes 10616832 | tf_op jit(solution)/shard_map/all_gather | solution.py:106
  69.8 21.8 %collective-permute-start.3 = (bf16[1,48,3072]{2,1,0:T(8,128)(2,1)S(1)}, bf16[1,48,3072]{2,1,0:T(8,128)(2,1)S(1)}, u32[]{:S(2)}, u32[]{:S(2)}) collective-permute-start(bf16[1,48,3072]{2,1,0:T(8,128)(2,1)S(1)} %pad_maximum_fusion.8), channel_id=1, source_target_pairs={{0,16},{8,24},{16,0},{24,8},{1,17},{9,25},{17,1},{25,9},{2,18},{10... | collective-permute-start | bytes 884744 | tf_op jit(solution)/shard_map/ppermute | solution.py:89
  76.5 56.3 %collective-permute-start.4 = (bf16[1,48,3072]{2,1,0:T(8,128)(2,1)S(1)}, bf16[1,48,3072]{2,1,0:T(8,128)(2,1)S(1)}, u32[]{:S(2)}, u32[]{:S(2)}) collective-permute-start(bf16[1,48,3072]{2,1,0:T(8,128)(2,1)S(1)} %pad_maximum_fusion.7), channel_id=1, source_target_pairs={{0,8},{8,16},{16,24},{24,0},{1,9},{9,17},{17,25},{25,1},{2,10},{10... | collective-permute-start | bytes 884744 | tf_op jit(solution)/shard_map/ppermute | solution.py:89
  84.4 48.4 %collective-permute-start.5 = (bf16[1,48,3072]{2,1,0:T(8,128)(2,1)S(1)}, bf16[1,48,3072]{2,1,0:T(8,128)(2,1)S(1)}, u32[]{:S(2)}, u32[]{:S(2)}) collective-permute-start(bf16[1,48,3072]{2,1,0:T(8,128)(2,1)S(1)} %pad_maximum_fusion.9), channel_id=1, source_target_pairs={{0,24},{8,0},{16,8},{24,16},{1,25},{9,1},{17,9},{25,17},{2,26},{10... | collective-permute-start | bytes 884744 | tf_op jit(solution)/shard_map/ppermute | solution.py:89
  134.0 0.7 copy-start.3
Sparse Core Ops, SparseCore 0:
  69.9 65.7 all-gather.2
  137.8 62.0 all-gather.4

commit v5 on v1

v5 whole, which is shorter than its diff:
```python
import jax
import jax.numpy as jnp
from jax import lax
from jax.experimental import pallas as pl
from jax.experimental.pallas import tpu as pltpu
from jax.sharding import Mesh, PartitionSpec as P

CAP = 3
CHUNKS = 8
STEPS = 4
AHEAD = 2
MIB = 1 << 20


def swiglu_kernel(x_ref, gate_ref, pair_ref, out_ref, gates, pairs, total, arrival):
    blocks, rows, width = gate_ref.shape
    group = blocks // STEPS
    copies = []
    for i in range(STEPS):
        part = pl.ds(i * group, group)
        copies.append(
            (
                pltpu.make_async_copy(gate_ref.at[part], gates.at[part], arrival.at[2 * i]),
                pltpu.make_async_copy(pair_ref.at[part], pairs.at[part], arrival.at[2 * i + 1]),
            )
        )
    for gate_copy, pair_copy in copies[:AHEAD]:
        gate_copy.start()
        pair_copy.start()
    across = (((1,), (1,)), ((), ()))

    def score(matrix):
        return lax.dot_general(x_ref[...], matrix, across, preferred_element_type=jnp.float32)

    for i, (gate_copy, pair_copy) in enumerate(copies):
        part = slice(i * group, (i + 1) * group)
        gate_copy.wait()
        pair_copy.wait()
        for gate_later, pair_later in copies[i + AHEAD : i + AHEAD + 1]:
            gate_later.start()
            pair_later.start()
        gate = score(gates[part].reshape(group * rows, width))
        up = score(pairs[part, :rows, :].reshape(group * rows, width))
        hidden = (gate / (1.0 + jnp.exp(-gate)) * up).astype(jnp.bfloat16)
        down = pairs[part, rows:, :].reshape(group * rows, width)
        product = jnp.dot(hidden, down, preferred_element_type=jnp.float32)
        if i == 0:
            total[...] = product
        elif i < STEPS - 1:
            total[...] += product
        else:
            out_ref[...] = (total[...] + product).astype(out_ref.dtype)


def swiglu(x, gate, pair):
    slots, width = x.shape
    units = gate.shape[0] * gate.shape[1]
    return pl.pallas_call(
        swiglu_kernel,
        out_shape=jax.ShapeDtypeStruct(x.shape, jnp.bfloat16),
        in_specs=[pl.BlockSpec(memory_space=pltpu.VMEM)]
        + [pl.BlockSpec(memory_space=pl.ANY)] * 2,
        out_specs=pl.BlockSpec(memory_space=pltpu.VMEM),
        scratch_shapes=[
            pltpu.VMEM(gate.shape, jnp.bfloat16),
            pltpu.VMEM(pair.shape, jnp.bfloat16),
            pltpu.VMEM((slots, width), jnp.float32),
            pltpu.SemaphoreType.DMA((2 * STEPS,)),
        ],
        compiler_params=pltpu.CompilerParams(vmem_limit_bytes=48 * MIB),
        cost_estimate=pl.CostEstimate(
            flops=6 * slots * units * width,
            bytes_accessed=6 * units * width + 4 * slots * width,
            transcendentals=slots * units,
        ),
    )(x, gate, pair)


def shards(tokens, expert_ids, gate_weight, up_weight, down_weight):
    exp_dev, _, width = gate_weight.shape
    routes = ("x", "zlo", "zhi")
    experts = exp_dev * lax.axis_size("x") * lax.axis_size("zlo")
    chunk = width // CHUNKS
    slots = experts * CAP

    def tied(*values):
        return lax.optimization_barrier(values)

    def over_z(payload):
        return lax.all_to_all(payload, "zhi", split_axis=0, concat_axis=0, tiled=True)

    def over_plane(part):
        return lax.all_gather(part, ("y", "core"), axis=0, tiled=True)

    late = jnp.concatenate([up_weight, down_weight], axis=1)
    first, late = tied(over_z(gate_weight), late)
    second = over_z(late)
    tokens, second = tied(tokens, second)
    first, second = over_plane(first), over_plane(second)

    flat_ids = expert_ids[:, 0]
    matches = (flat_ids[:, None] == jnp.arange(experts, dtype=jnp.int32)[None, :]).astype(jnp.int32)
    rank_of = jnp.sum((jnp.cumsum(matches, axis=0) - 1) * matches, axis=1)
    position = flat_ids * CAP + rank_of
    selector = (position[None, :] == jnp.arange(slots, dtype=jnp.int32)[:, None]).astype(jnp.bfloat16)
    packed = jnp.dot(selector, tokens, preferred_element_type=jnp.float32).astype(jnp.bfloat16)
    packed = packed.reshape(experts, CAP * CHUNKS, chunk)
    arrived = lax.all_to_all(packed, routes, split_axis=0, concat_axis=0, tiled=True)

    result = swiglu(arrived.reshape(slots, width), first, second)
    result = result.reshape(experts, CAP * CHUNKS, chunk)
    returned = lax.all_to_all(result, routes, split_axis=0, concat_axis=0, tiled=True)
    returned = returned.reshape(slots, width)
    output = lax.dot_general(
        selector, returned, (((0,), (0,)), ((), ())), preferred_element_type=jnp.float32
    )
    return output.astype(jnp.bfloat16)


def solution(mesh):
    fine = Mesh(mesh.devices.reshape(4, 4, 4, 4, 2), ("x", "zlo", "zhi", "y", "core"))
    everyone = ("x", "zlo", "zhi", "y", "core")
    group = ("x", "zlo")
    sub = ("zhi", "y", "core")
    return jax.shard_map(
        shards,
        mesh=fine,
        in_specs=(
            P(everyone, None),
            P(everyone, None),
            P(group, sub, None),
            P(group, sub, None),
            P(group, sub, None),
        ),
        out_specs=P(everyone, None),
        check_vma=False,
    )
```

time: 306 us -> 305 us (level)
  the two profiles are of different devices: /device:TPU:56 before, /device:TPU:32 now
where the time goes in v5:
time: 305 us; the launch traced here: 304 us
  blocking collectives  223 us (73%)
  waiting for transfers between devices  37.5 us (12%)
  starting transfers between devices  14.4 us (5%)
  between operations  13.5 us (4%)
  Pallas kernels  8.65 us (3%)
  local copies, waits for them, and re-layouts  3.83 us (1%)
    all_to_all x1, blocking collectives, over_z(): lax.all_to_all(payload, 'zhi', split_axis=0, concat_axis=0, tiled=True)  81.6 us
    all_to_all x1, blocking collectives, shards(): lax.all_to_all(result, routes, split_axis=0, concat_axis=0, tiled=True)  73.6 us
    all_to_all x1, blocking collectives, shards(): lax.all_to_all(packed, routes, split_axis=0, concat_axis=0, tiled=True)  67.7 us
    all_to_all x1, waiting for transfers between devices, over_z(): lax.all_to_all(payload, 'zhi', split_axis=0, concat_axis=0, tiled=True)  37.5 us
    all_to_all x1, starting transfers between devices, over_z(): lax.all_to_all(payload, 'zhi', split_axis=0, concat_axis=0, tiled=True)  14.3 us
    pallas_call x1, Pallas kernels, swiglu(): pl.pallas_call(swiglu_kernel, out_shape=jax.ShapeDtypeStruct(x.shape, jnp...  8.65 us
  transfers between devices with their start and end apart: 3, of which 1 were waited for; matrix products, arithmetic and copies ran while one was open for 1% of the time, Pallas kernels for 0%

profile of v5, /device:TPU:32, one launch (start us, length us, event | category | flops | bytes accessed | tf_op | source)
XLA Modules:
  0.0 304.5 jit_solution(4188687576221694329)
XLA Ops:
  6.5 0.0 copy-start
  6.5 14.3 %all-to-all-start = ((bf16[4,32,3072]{2,1,0:T(8,128)(2,1)}), bf16[4,32,3072]{2,1,0:T(8,128)(2,1)S(1)}, u32[]{:S(2)}, u32[]{:S(2)}) async-start(bf16[4,32,3072]{2,1,0:T(8,128)(2,1)} %param.7), calls=%async_computation | async-start | bytes 1572864 | tf_op jit(solution)/shard_map/all_to_all | solution.py:90
  20.9 0.0 all-gather.3.cloned.1.call-start
  20.9 1.5 pad_maximum_fusion
  22.3 37.5 %all-to-all-done = bf16[4,32,3072]{2,1,0:T(8,128)(2,1)S(1)} async-done(((bf16[4,32,3072]{2,1,0:T(8,128)(2,1)}), bf16[4,32,3072]{2,1,0:T(8,128)(2,1)S(1)}, u32[]{:S(2)}, u32[]{:S(2)}) %all-to-all-start) | async-done | bytes 786464 | tf_op jit(solution)/shard_map/all_to_all | solution.py:90
  59.8 0.0 copy-start.1
  59.8 0.9 copy-done.1
  60.7 0.0 all-gather.3.cloned.1.call-update
  60.7 0.0 all-gather.5.cloned.1.call-start
  60.8 81.6 %all_to_all.20 = bf16[4,64,3072]{2,1,0:T(8,128)(2,1)} all-to-all(bf16[4,64,3072]{2,1,0:T(8,128)(2,1)S(1)} %pad_maximum_fusion), channel_id=1, replica_groups=mesh['x'=4,'zlo'=4,'zhi'=4,'y'=4,'core'=2] {'zhi'}, dimensions={0} | all-to-all | bytes 3145728 | tf_op jit(solution)/shard_map/all_to_all | solution.py:90
  142.4 0.0 copy-start.2
  142.4 0.0 all-gather.5.cloned.1.call-update
  142.4 0.6 copy-done.2
  143.1 0.1 fusion
  143.1 0.2 reduce_window_sum.11
  143.3 0.2 select_reduce_fusion
  143.5 0.0 copy-done
  143.5 0.5 convolution_convert_fusion
  144.0 0.6 reshape.20
  144.6 67.7 %all_to_all.21 = bf16[64,24,384]{2,1,0:T(8,128)(2,1)S(1)} all-to-all(bf16[64,24,384]{2,1,0:T(8,128)(2,1)S(1)} %reshape.20), channel_id=1, replica_groups=mesh['x'=4,'zlo'=4,'zhi'=4,'y'=4,'core'=2] {'x','zlo','zhi'}, dimensions={0} | all-to-all | bytes 2359296 | tf_op jit(solution)/shard_map/all_to_all | solution.py:108
  212.3 0.6 reshape.21.x_ref
  212.9 0.0 all-gather.3.cloned.1.call-done.gate_ref
  212.9 0.0 all-gather.5.cloned.1.call-done.pair_ref
  212.9 8.7 %shard_map.55 = bf16[192,3072]{1,0:T(8,128)(2,1)S(1)} custom-call(bf16[192,3072]{1,0:T(8,128)(2,1)S(1)} %reshape.21.x_ref, bf16[32,32,3072]{2,1,0:T(8,128)(2,1)} %all-gather.3.cloned.1.call-done.gate_ref, bf16[32,64,3072]{2,1,0:T(8,128)(2,1)} %all-gather.5.cloned.1.call-done.pair_ref), custom_call_target="tpu_custom_call" | custom-call | flops 3623878656 | bytes 21233664 | tf_op jit(solution)/shard_map/pallas_call | solution.py:58
  221.6 0.6 reshape.22
  222.2 73.6 %all_to_all.22 = bf16[64,24,384]{2,1,0:T(8,128)(2,1)S(1)} all-to-all(bf16[64,24,384]{2,1,0:T(8,128)(2,1)S(1)} %reshape.22), channel_id=1, replica_groups=mesh['x'=4,'zlo'=4,'zhi'=4,'y'=4,'core'=2] {'x','zlo','zhi'}, dimensions={0} | all-to-all | bytes 2359296 | tf_op jit(solution)/shard_map/all_to_all | solution.py:112
  295.8 0.6 reshape.23
  296.3 1.3 convolution_convert_fusion.1
  (1 shorter events, 0.0 us)
Async XLA Ops:
  6.5 137.0 %copy-start = (bf16[128,3072]{1,0:T(8,128)(2,1)S(1)}, bf16[128,3072]{1,0:T(8,128)(2,1)}, u32[]{:S(2)}) copy-start(bf16[128,3072]{1,0:T(8,128)(2,1)} %param.5) | copy-start | bytes 2359300
  6.5 53.3 %all-to-all-start = ((bf16[4,32,3072]{2,1,0:T(8,128)(2,1)}), bf16[4,32,3072]{2,1,0:T(8,128)(2,1)S(1)}, u32[]{:S(2)}, u32[]{:S(2)}) async-start(bf16[4,32,3072]{2,1,0:T(8,128)(2,1)} %param.7), calls=%async_computation | async-start | bytes 1572864 | tf_op jit(solution)/shard_map/all_to_all | solution.py:90
  20.9 192.0 %all-gather.3.cloned.1.call-start = ((), (), s32[]{:S(2)}) async-start(), calls=%async_computation.4 | async-start | bytes 7077888 | tf_op jit(solution)/shard_map/all_gather | solution.py:93
  59.8 0.9 copy-start.1
  60.7 152.2 %all-gather.5.cloned.1.call-start = ((), (), s32[]{:S(2)}) async-start(), calls=%async_computation.5 | async-start | bytes 14155776 | tf_op jit(solution)/shard_map/all_gather | solution.py:93
  142.4 0.7 copy-start.2
Sparse Core Ops, SparseCore 0:
  60.8 46.2 all-gather.2
  142.5 68.6 all-gather.4

commit v6 on v4

--- a/solution.py
+++ b/solution.py
@@ -113,8 +113,6 @@
     first = joined(tied(*over_z(list(early))))
     first, *late = tied(first, *late)
     second = joined(tied(*over_z(late)))
-    tokens, second = tied(tokens, second)
-    first, second = over_plane(first), over_plane(second)
 
     flat_ids = expert_ids[:, 0]
     matches = (flat_ids[:, None] == jnp.arange(experts, dtype=jnp.int32)[None, :]).astype(jnp.int32)
@@ -122,8 +120,16 @@
     position = flat_ids * CAP + rank_of
     selector = (position[None, :] == jnp.arange(slots, dtype=jnp.int32)[:, None]).astype(jnp.bfloat16)
     packed = jnp.dot(selector, tokens, preferred_element_type=jnp.float32).astype(jnp.bfloat16)
-    packed = packed.reshape(experts, CAP * CHUNKS, chunk)
-    arrived = lax.all_to_all(packed, routes, split_axis=0, concat_axis=0, tiled=True)
+    columns = lax.axis_size("x")
+    depth = experts // columns
+    message = CAP * CHUNKS
+    packed = packed.reshape(columns, depth * message, chunk)
+    packed = lax.all_to_all(packed, "x", split_axis=0, concat_axis=0, tiled=True)
+    packed = packed.reshape(columns, depth, message, chunk).swapaxes(0, 1)
+    packed, second = tied(packed.reshape(depth, columns * message, chunk), second)
+    first, second = over_plane(first), over_plane(second)
+    arrived = lax.all_to_all(packed, ("zlo", "zhi"), split_axis=0, concat_axis=0, tiled=True)
+    arrived = arrived.reshape(depth, columns, message, chunk).swapaxes(0, 1)
 
     result = swiglu(arrived.reshape(slots, width), [first, second])
     result = result.reshape(experts, CAP * CHUNKS, chunk)

time: 294 us -> 295 us (level)
  starting transfers between devices: 46.4 us -> 50.6 us
  blocking collectives: 139 us -> 135 us
    all_to_all x0 -> x1, starting transfers between devices: none -> 4.29 us  [shards(): lax.all_to_all(packed, 'x', split_axis=0, concat_axis=0, tiled=True)]
    all_to_all x1, blocking collectives: 72.2 us -> 68.7 us  [shards(): lax.all_to_all(packed, ('zlo', 'zhi'), split_axis=0, concat_axis=0, tiled...]
  transfers between devices with their start and end apart: 8 -> 9, of which waited for: 3 -> 3; matrix products, arithmetic and copies ran while one was open for 1% -> 1% of each run, Pallas kernels for 0% -> 0%
where the time goes in v6:
time: 295 us
  blocking collectives  135 us (46%)
  waiting for transfers between devices  76.2 us (26%)
  starting transfers between devices  50.6 us (17%)
  between operations  13.6 us (5%)
  Pallas kernels  8.62 us (3%)
  local copies, waits for them, and re-layouts  5.9 us (2%)
  other arithmetic  2.95 us (1%)
    ppermute x6, waiting for transfers between devices, shifted(): lax.ppermute(value, axis, [(i, (i + step) % size) for i in range(size)])  76.2 us
    all_to_all x1, blocking collectives, shards(): lax.all_to_all(packed, ('zlo', 'zhi'), split_axis=0, concat_axis=0, tiled...  68.7 us
    all_to_all x1, blocking collectives, shards(): lax.all_to_all(result, routes, split_axis=0, concat_axis=0, tiled=True)  66.6 us
    ppermute x6, starting transfers between devices, shifted(): lax.ppermute(value, axis, [(i, (i + step) % size) for i in range(size)])  46.3 us
    pallas_call x1, Pallas kernels, swiglu(): pl.pallas_call(swiglu_kernel, out_shape=jax.ShapeDtypeStruct(x.shape, jnp...  8.62 us
  transfers between devices with their start and end apart: 9, of which 3 were waited for; matrix products, arithmetic and copies ran while one was open for 1% of the time, Pallas kernels for 0%

profile of v6, /device:TPU:32, one launch (start us, length us, event | category | flops | bytes accessed | tf_op | source)
XLA Modules:
  0.0 295.0 jit_solution(16042227531572027483)
XLA Ops:
  6.5 0.0 copy-start
  6.5 0.0 copy-start.2
  6.5 0.0 copy-start.1
  6.5 0.0 all-gather.3.cloned.1.call-start
  6.6 1.4 constant_dynamic-slice_fusion.23
  8.0 0.1 copy-done.2
  8.1 0.2 copy-done.1
  8.3 0.1 constant_dynamic-slice_fusion
  8.6 14.8 %collective-permute-start = (bf16[1,48,3072]{2,1,0:T(8,128)(2,1)S(1)}, bf16[1,48,3072]{2,1,0:T(8,128)(2,1)S(1)}, u32[]{:S(2)}, u32[]{:S(2)}) collective-permute-start(bf16[1,48,3072]{2,1,0:T(8,128)(2,1)S(1)} %pad_maximum_fusion.4), channel_id=1, source_target_pairs={{0,16},{8,24},{16,0},{24,8},{1,17},{9,25},{17,1},{25,9},{2,18},{10... | collective-permute-start | bytes 884744 | tf_op jit(solution)/shard_map/ppermute | solution.py:89
  23.4 4.3 %collective-permute-start.1 = (bf16[1,48,3072]{2,1,0:T(8,128)(2,1)S(1)}, bf16[1,48,3072]{2,1,0:T(8,128)(2,1)S(1)}, u32[]{:S(2)}, u32[]{:S(2)}) collective-permute-start(bf16[1,48,3072]{2,1,0:T(8,128)(2,1)S(1)} %pad_maximum_fusion.3), channel_id=1, source_target_pairs={{0,8},{8,16},{16,24},{24,0},{1,9},{9,17},{17,25},{25,1},{2,10},{10... | collective-permute-start | bytes 884744 | tf_op jit(solution)/shard_map/ppermute | solution.py:89
  27.7 5.5 %collective-permute-start.2 = (bf16[1,48,3072]{2,1,0:T(8,128)(2,1)S(1)}, bf16[1,48,3072]{2,1,0:T(8,128)(2,1)S(1)}, u32[]{:S(2)}, u32[]{:S(2)}) collective-permute-start(bf16[1,48,3072]{2,1,0:T(8,128)(2,1)S(1)} %pad_maximum_fusion.5), channel_id=1, source_target_pairs={{0,24},{8,0},{16,8},{24,16},{1,25},{9,1},{17,9},{25,17},{2,26},{10... | collective-permute-start | bytes 884744 | tf_op jit(solution)/shard_map/ppermute | solution.py:89
  33.3 26.0 %collective-permute-done = bf16[1,48,3072]{2,1,0:T(8,128)(2,1)S(1)} collective-permute-done((bf16[1,48,3072]{2,1,0:T(8,128)(2,1)S(1)}, bf16[1,48,3072]{2,1,0:T(8,128)(2,1)S(1)}, u32[]{:S(2)}, u32[]{:S(2)}) %collective-permute-start) | collective-permute-done | bytes 294944 | tf_op jit(solution)/shard_map/ppermute | solution.py:89
  59.2 0.0 collective-permute-done.1
  59.3 9.3 %collective-permute-done.2 = bf16[1,48,3072]{2,1,0:T(8,128)(2,1)S(1)} collective-permute-done((bf16[1,48,3072]{2,1,0:T(8,128)(2,1)S(1)}, bf16[1,48,3072]{2,1,0:T(8,128)(2,1)S(1)}, u32[]{:S(2)}, u32[]{:S(2)}) %collective-permute-start.2) | collective-permute-done | bytes 294944 | tf_op jit(solution)/shard_map/ppermute | solution.py:89
  68.6 1.2 pad_maximum_fusion
  69.8 0.0 copy-start.3
  69.8 0.0 all-gather.3.cloned.1.call-update
  69.8 0.6 copy-done.3
  70.4 0.1 fusion
  70.5 0.2 reduce_window_sum.11
  70.7 0.2 select_reduce_fusion
  70.9 0.0 copy-done
  70.9 0.5 convolution_convert_fusion
  71.4 1.4 reshape.29
  72.8 4.3 %all-to-all-start = ((bf16[4,384,384]{2,1,0:T(8,128)(2,1)}), bf16[4,384,384]{2,1,0:T(8,128)(2,1)S(1)}, u32[]{:S(2)}, u32[]{:S(2)}) async-start(bf16[4,384,384]{2,1,0:T(8,128)(2,1)} %reshape.29), calls=%async_computation | async-start | bytes 2359296 | tf_op jit(solution)/shard_map/all_to_all | solution.py:127
  77.1 0.0 all-gather.5.cloned.1.call-start
  77.1 6.6 %collective-permute-start.3 = (bf16[1,48,3072]{2,1,0:T(8,128)(2,1)S(1)}, bf16[1,48,3072]{2,1,0:T(8,128)(2,1)S(1)}, u32[]{:S(2)}, u32[]{:S(2)}) collective-permute-start(bf16[1,48,3072]{2,1,0:T(8,128)(2,1)S(1)} %pad_maximum_fusion.8), channel_id=1, source_target_pairs={{0,16},{8,24},{16,0},{24,8},{1,17},{9,25},{17,1},{25,9},{2,18},{10... | collective-permute-start | bytes 884744 | tf_op jit(solution)/shard_map/ppermute | solution.py:89
  83.7 8.0 %collective-permute-start.4 = (bf16[1,48,3072]{2,1,0:T(8,128)(2,1)S(1)}, bf16[1,48,3072]{2,1,0:T(8,128)(2,1)S(1)}, u32[]{:S(2)}, u32[]{:S(2)}) collective-permute-start(bf16[1,48,3072]{2,1,0:T(8,128)(2,1)S(1)} %pad_maximum_fusion.7), channel_id=1, source_target_pairs={{0,8},{8,16},{16,24},{24,0},{1,9},{9,17},{17,25},{25,1},{2,10},{10... | collective-permute-start | bytes 884744 | tf_op jit(solution)/shard_map/ppermute | solution.py:89
  91.7 7.2 %collective-permute-start.5 = (bf16[1,48,3072]{2,1,0:T(8,128)(2,1)S(1)}, bf16[1,48,3072]{2,1,0:T(8,128)(2,1)S(1)}, u32[]{:S(2)}, u32[]{:S(2)}) collective-permute-start(bf16[1,48,3072]{2,1,0:T(8,128)(2,1)S(1)} %pad_maximum_fusion.9), channel_id=1, source_target_pairs={{0,24},{8,0},{16,8},{24,16},{1,25},{9,1},{17,9},{25,17},{2,26},{10... | collective-permute-start | bytes 884744 | tf_op jit(solution)/shard_map/ppermute | solution.py:89
  98.9 0.0 collective-permute-done.3
  98.9 40.8 %collective-permute-done.4 = bf16[1,48,3072]{2,1,0:T(8,128)(2,1)S(1)} collective-permute-done((bf16[1,48,3072]{2,1,0:T(8,128)(2,1)S(1)}, bf16[1,48,3072]{2,1,0:T(8,128)(2,1)S(1)}, u32[]{:S(2)}, u32[]{:S(2)}) %collective-permute-start.4) | collective-permute-done | bytes 294944 | tf_op jit(solution)/shard_map/ppermute | solution.py:89
  139.7 0.0 collective-permute-done.5
  139.7 1.2 pad_maximum_fusion.1
  140.9 0.0 all-to-all-done
  140.9 0.1 copy.9
  141.0 0.0 all-gather.5.cloned.1.call-update
  141.0 68.7 %all_to_all.15 = bf16[16,96,384]{2,1,0:T(8,128)(2,1)S(1)} all-to-all(bf16[16,96,384]{2,1,0:T(8,128)(2,1)S(1)} %bitcast.14), channel_id=1, replica_groups=mesh['x'=4,'zlo'=4,'zhi'=4,'y'=4,'core'=2] {'zlo','zhi'}, dimensions={0} | all-to-all | bytes 2359296 | tf_op jit(solution)/shard_map/all_to_all | solution.py:131
  209.7 0.1 copy.10
  209.8 0.6 reshape.33.x_ref
  210.4 0.0 all-gather.3.cloned.1.call-done.refs_0_
  210.5 0.0 all-gather.5.cloned.1.call-done.refs_1_
  210.5 8.6 %shard_map.55 = bf16[192,3072]{1,0:T(8,128)(2,1)S(1)} custom-call(bf16[192,3072]{1,0:T(8,128)(2,1)S(1)} %reshape.33.x_ref, bf16[32,48,3072]{2,1,0:T(8,128)(2,1)} %all-gather.3.cloned.1.call-done.refs_0_, bf16[32,48,3072]{2,1,0:T(8,128)(2,1)} %all-gather.5.cloned.1.call-done.refs_1_), custom_call_target="tpu_custom_call" | custom-call | flops 3623878656 | bytes 21233664 | tf_op jit(solution)/shard_map/pallas_call | solution.py:54
  219.1 0.6 reshape.34
  219.7 66.6 %all_to_all.16 = bf16[64,24,384]{2,1,0:T(8,128)(2,1)S(1)} all-to-all(bf16[64,24,384]{2,1,0:T(8,128)(2,1)S(1)} %reshape.34), channel_id=1, replica_groups=mesh['x'=4,'zlo'=4,'zhi'=4,'y'=4,'core'=2] {'x','zlo','zhi'}, dimensions={0} | all-to-all | bytes 2359296 | tf_op jit(solution)/shard_map/all_to_all | solution.py:136
  286.3 0.6 reshape.35
  286.9 1.3 convolution_convert_fusion.1
  (9 shorter events, 0.2 us)
Async XLA Ops:
  6.5 64.3 %copy-start = (bf16[128,3072]{1,0:T(8,128)(2,1)S(1)}, bf16[128,3072]{1,0:T(8,128)(2,1)}, u32[]{:S(2)}) copy-start(bf16[128,3072]{1,0:T(8,128)(2,1)} %param.5) | copy-start | bytes 2359300
  6.5 1.5 copy-start.2
  6.5 1.8 copy-start.1
  6.5 203.9 %all-gather.3.cloned.1.call-start = ((), (), s32[]{:S(2)}) async-start(), calls=%async_computation.3 | async-start | bytes 10616832 | tf_op jit(solution)/shard_map/all_gather | solution.py:106
  8.6 50.7 %collective-permute-start = (bf16[1,48,3072]{2,1,0:T(8,128)(2,1)S(1)}, bf16[1,48,3072]{2,1,0:T(8,128)(2,1)S(1)}, u32[]{:S(2)}, u32[]{:S(2)}) collective-permute-start(bf16[1,48,3072]{2,1,0:T(8,128)(2,1)S(1)} %pad_maximum_fusion.4), channel_id=1, source_target_pairs={{0,16},{8,24},{16,0},{24,8},{1,17},{9,25},{17,1},{25,9},{2,18},{10... | collective-permute-start | bytes 884744 | tf_op jit(solution)/shard_map/ppermute | solution.py:89
  23.4 35.9 %collective-permute-start.1 = (bf16[1,48,3072]{2,1,0:T(8,128)(2,1)S(1)}, bf16[1,48,3072]{2,1,0:T(8,128)(2,1)S(1)}, u32[]{:S(2)}, u32[]{:S(2)}) collective-permute-start(bf16[1,48,3072]{2,1,0:T(8,128)(2,1)S(1)} %pad_maximum_fusion.3), channel_id=1, source_target_pairs={{0,8},{8,16},{16,24},{24,0},{1,9},{9,17},{17,25},{25,1},{2,10},{10... | collective-permute-start | bytes 884744 | tf_op jit(solution)/shard_map/ppermute | solution.py:89
  27.7 40.9 %collective-permute-start.2 = (bf16[1,48,3072]{2,1,0:T(8,128)(2,1)S(1)}, bf16[1,48,3072]{2,1,0:T(8,128)(2,1)S(1)}, u32[]{:S(2)}, u32[]{:S(2)}) collective-permute-start(bf16[1,48,3072]{2,1,0:T(8,128)(2,1)S(1)} %pad_maximum_fusion.5), channel_id=1, source_target_pairs={{0,24},{8,0},{16,8},{24,16},{1,25},{9,1},{17,9},{25,17},{2,26},{10... | collective-permute-start | bytes 884744 | tf_op jit(solution)/shard_map/ppermute | solution.py:89
  69.8 0.7 copy-start.3
  72.8 68.1 %all-to-all-start = ((bf16[4,384,384]{2,1,0:T(8,128)(2,1)}), bf16[4,384,384]{2,1,0:T(8,128)(2,1)S(1)}, u32[]{:S(2)}, u32[]{:S(2)}) async-start(bf16[4,384,384]{2,1,0:T(8,128)(2,1)} %reshape.29), calls=%async_computation | async-start | bytes 2359296 | tf_op jit(solution)/shard_map/all_to_all | solution.py:127
  77.1 133.4 %all-gather.5.cloned.1.call-start = ((), (), s32[]{:S(2)}) async-start(), calls=%async_computation.4 | async-start | bytes 10616832 | tf_op jit(solution)/shard_map/all_gather | solution.py:106
  77.1 21.8 %collective-permute-start.3 = (bf16[1,48,3072]{2,1,0:T(8,128)(2,1)S(1)}, bf16[1,48,3072]{2,1,0:T(8,128)(2,1)S(1)}, u32[]{:S(2)}, u32[]{:S(2)}) collective-permute-start(bf16[1,48,3072]{2,1,0:T(8,128)(2,1)S(1)} %pad_maximum_fusion.8), channel_id=1, source_target_pairs={{0,16},{8,24},{16,0},{24,8},{1,17},{9,25},{17,1},{25,9},{2,18},{10... | collective-permute-start | bytes 884744 | tf_op jit(solution)/shard_map/ppermute | solution.py:89
  83.7 56.0 %collective-permute-start.4 = (bf16[1,48,3072]{2,1,0:T(8,128)(2,1)S(1)}, bf16[1,48,3072]{2,1,0:T(8,128)(2,1)S(1)}, u32[]{:S(2)}, u32[]{:S(2)}) collective-permute-start(bf16[1,48,3072]{2,1,0:T(8,128)(2,1)S(1)} %pad_maximum_fusion.7), channel_id=1, source_target_pairs={{0,8},{8,16},{16,24},{24,0},{1,9},{9,17},{17,25},{25,1},{2,10},{10... | collective-permute-start | bytes 884744 | tf_op jit(solution)/shard_map/ppermute | solution.py:89
  91.7 48.0 %collective-permute-start.5 = (bf16[1,48,3072]{2,1,0:T(8,128)(2,1)S(1)}, bf16[1,48,3072]{2,1,0:T(8,128)(2,1)S(1)}, u32[]{:S(2)}, u32[]{:S(2)}) collective-permute-start(bf16[1,48,3072]{2,1,0:T(8,128)(2,1)S(1)} %pad_maximum_fusion.9), channel_id=1, source_target_pairs={{0,24},{8,0},{16,8},{24,16},{1,25},{9,1},{17,9},{25,17},{2,26},{10... | collective-permute-start | bytes 884744 | tf_op jit(solution)/shard_map/ppermute | solution.py:89
Sparse Core Ops, SparseCore 0:
  69.9 65.7 all-gather.2
  141.2 60.2 all-gather.4

commit v7 on v6

--- a/solution.py
+++ b/solution.py
@@ -108,12 +108,6 @@
     def joined(pieces):
         return jnp.concatenate(pieces, axis=0)
 
-    early = tied(*[outgoing(step, 0) for step in range(ring)])
-    late = tied(*[outgoing(step, 1) for step in range(ring)])
-    first = joined(tied(*over_z(list(early))))
-    first, *late = tied(first, *late)
-    second = joined(tied(*over_z(late)))
-
     flat_ids = expert_ids[:, 0]
     matches = (flat_ids[:, None] == jnp.arange(experts, dtype=jnp.int32)[None, :]).astype(jnp.int32)
     rank_of = jnp.sum((jnp.cumsum(matches, axis=0) - 1) * matches, axis=1)
@@ -126,6 +120,11 @@
     packed = packed.reshape(columns, depth * message, chunk)
     packed = lax.all_to_all(packed, "x", split_axis=0, concat_axis=0, tiled=True)
     packed = packed.reshape(columns, depth, message, chunk).swapaxes(0, 1)
+    early = tied(*[outgoing(step, 0) for step in range(ring)])
+    late = tied(*[outgoing(step, 1) for step in range(ring)])
+    first = joined(tied(*over_z(list(early))))
+    first, packed, *late = tied(first, packed, *late)
+    second = joined(tied(*over_z(late)))
     packed, second = tied(packed.reshape(depth, columns * message, chunk), second)
     first, second = over_plane(first), over_plane(second)
     arrived = lax.all_to_all(packed, ("zlo", "zhi"), split_axis=0, concat_axis=0, tiled=True)

time: 295 us -> 298 us (1.010)
  other arithmetic: 2.95 us -> 10.2 us
  starting transfers between devices: 50.6 us -> 45.5 us
  blocking collectives: 135 us -> 140 us
  waiting for transfers between devices: 76.2 us -> 71.6 us
    concatenate x8, other arithmetic: 0.17 us -> 6.29 us  [outgoing(): jnp.concatenate([lax.dynamic_slice(w, (target, part * part_rows, 0), (1,...]
    ppermute x6, starting transfers between devices: 46.3 us -> 41.1 us  [shifted(): lax.ppermute(value, axis, [(i, (i + step) % size) for i in range(size)])]
    all_to_all x1, blocking collectives: 66.6 us -> 71.7 us  [shards(): lax.all_to_all(result, routes, split_axis=0, concat_axis=0, tiled=True)]
    ppermute x6, waiting for transfers between devices: 76.2 us -> 71.5 us  [shifted(): lax.ppermute(value, axis, [(i, (i + step) % size) for i in range(size)])]
  transfers between devices with their start and end apart: 9 -> 9, of which waited for: 3 -> 4; matrix products, arithmetic and copies ran while one was open for 1% -> 4% of each run, Pallas kernels for 0% -> 0%
where the time goes in v7:
time: 298 us; the launch traced here: 297 us
  blocking collectives  140 us (47%)
  waiting for transfers between devices  71.6 us (24%)
  starting transfers between devices  45.5 us (15%)
  between operations  13.6 us (5%)
  other arithmetic  10.2 us (3%)
  Pallas kernels  8.61 us (3%)
  local copies, waits for them, and re-layouts  5.65 us (2%)
    all_to_all x1, blocking collectives, shards(): lax.all_to_all(result, routes, split_axis=0, concat_axis=0, tiled=True)  71.7 us
    ppermute x6, waiting for transfers between devices, shifted(): lax.ppermute(value, axis, [(i, (i + step) % size) for i in range(size)])  71.5 us
    all_to_all x1, blocking collectives, shards(): lax.all_to_all(packed, ('zlo', 'zhi'), split_axis=0, concat_axis=0, tiled...  68.7 us
    ppermute x6, starting transfers between devices, shifted(): lax.ppermute(value, axis, [(i, (i + step) % size) for i in range(size)])  41.1 us
    pallas_call x1, Pallas kernels, swiglu(): pl.pallas_call(swiglu_kernel, out_shape=jax.ShapeDtypeStruct(x.shape, jnp...  8.61 us
    concatenate x8, other arithmetic, outgoing(): jnp.concatenate([lax.dynamic_slice(w, (target, part * part_rows, 0), (1,...  6.29 us
  transfers between devices with their start and end apart: 9, of which 4 were waited for; matrix products, arithmetic and copies ran while one was open for 4% of the time, Pallas kernels for 0%

profile of v7, /device:TPU:32, one launch (start us, length us, event | category | flops | bytes accessed | tf_op | source)
XLA Modules:
  0.0 297.2 jit_solution(12166827395777709550)
XLA Ops:
  6.5 0.0 copy-start
  6.5 0.0 copy-start.2
  6.5 0.0 copy-start.1
  6.5 2.1 constant_dynamic-slice_fusion.23
  8.7 0.0 copy-done.2
  8.7 0.0 copy-done.1
  8.7 0.1 constant_dynamic-slice_fusion
  8.8 0.0 copy-start.4
  8.8 0.7 pad_maximum_fusion.5
  9.6 0.7 pad_maximum_fusion.4
  10.3 0.7 pad_maximum_fusion.3
  11.1 14.8 %collective-permute-start = (bf16[1,48,3072]{2,1,0:T(8,128)(2,1)}, bf16[1,48,3072]{2,1,0:T(8,128)(2,1)}, u32[]{:S(2)}, u32[]{:S(2)}) collective-permute-start(bf16[1,48,3072]{2,1,0:T(8,128)(2,1)} %pad_maximum_fusion.4), channel_id=1, source_target_pairs={{0,16},{8,24},{16,0},{24,8},{1,17},{9,25},{17,1},{25,9},{2,18},{10... | collective-permute-start | bytes 884744 | tf_op jit(solution)/shard_map/ppermute | solution.py:89
  25.9 4.3 %collective-permute-start.1 = (bf16[1,48,3072]{2,1,0:T(8,128)(2,1)}, bf16[1,48,3072]{2,1,0:T(8,128)(2,1)}, u32[]{:S(2)}, u32[]{:S(2)}) collective-permute-start(bf16[1,48,3072]{2,1,0:T(8,128)(2,1)} %pad_maximum_fusion.3), channel_id=1, source_target_pairs={{0,8},{8,16},{16,24},{24,0},{1,9},{9,17},{17,25},{25,1},{2,10},{10... | collective-permute-start | bytes 884744 | tf_op jit(solution)/shard_map/ppermute | solution.py:89
  30.2 5.5 %collective-permute-start.2 = (bf16[1,48,3072]{2,1,0:T(8,128)(2,1)}, bf16[1,48,3072]{2,1,0:T(8,128)(2,1)}, u32[]{:S(2)}, u32[]{:S(2)}) collective-permute-start(bf16[1,48,3072]{2,1,0:T(8,128)(2,1)} %pad_maximum_fusion.5), channel_id=1, source_target_pairs={{0,24},{8,0},{16,8},{24,16},{1,25},{9,1},{17,9},{25,17},{2,26},{10... | collective-permute-start | bytes 884744 | tf_op jit(solution)/shard_map/ppermute | solution.py:89
  35.7 0.0 copy-done.4
  35.7 0.1 fusion
  35.8 0.2 reduce_window_sum.11
  35.9 0.2 select_reduce_fusion
  36.1 0.0 copy-done
  36.1 0.5 convolution_convert_fusion
  36.6 1.4 reshape.29
  38.0 4.3 %all-to-all-start = ((bf16[4,384,384]{2,1,0:T(8,128)(2,1)}), bf16[4,384,384]{2,1,0:T(8,128)(2,1)S(1)}, u32[]{:S(2)}, u32[]{:S(2)}) async-start(bf16[4,384,384]{2,1,0:T(8,128)(2,1)} %reshape.29), calls=%async_computation | async-start | bytes 2359296 | tf_op jit(solution)/shard_map/all_to_all | solution.py:121
  42.3 0.0 copy-start.3
  42.3 0.0 all-gather.3.cloned.1.call-start
  42.3 0.9 pad_maximum_fusion.6
  43.2 1.6 pad_maximum_fusion.7
  44.9 0.0 copy-done.3
  44.9 0.7 pad_maximum_fusion.8
  45.6 0.7 pad_maximum_fusion.9
  46.3 15.7 %collective-permute-done = bf16[1,48,3072]{2,1,0:T(8,128)(2,1)} collective-permute-done((bf16[1,48,3072]{2,1,0:T(8,128)(2,1)}, bf16[1,48,3072]{2,1,0:T(8,128)(2,1)}, u32[]{:S(2)}, u32[]{:S(2)}) %collective-permute-start) | collective-permute-done | bytes 294944 | tf_op jit(solution)/shard_map/ppermute | solution.py:89
  62.0 0.0 collective-permute-done.1
  62.0 9.4 %collective-permute-done.2 = bf16[1,48,3072]{2,1,0:T(8,128)(2,1)} collective-permute-done((bf16[1,48,3072]{2,1,0:T(8,128)(2,1)}, bf16[1,48,3072]{2,1,0:T(8,128)(2,1)}, u32[]{:S(2)}, u32[]{:S(2)}) %collective-permute-start.2) | collective-permute-done | bytes 294944 | tf_op jit(solution)/shard_map/ppermute | solution.py:89
  71.4 2.3 pad_maximum_fusion
  73.7 0.0 all-to-all-done
  73.7 0.0 all-gather.3.cloned.1.call-update
  73.8 0.0 all-gather.5.cloned.1.call-start
  73.8 6.6 %collective-permute-start.3 = (bf16[1,48,3072]{2,1,0:T(8,128)(2,1)}, bf16[1,48,3072]{2,1,0:T(8,128)(2,1)S(1)}, u32[]{:S(2)}, u32[]{:S(2)}) collective-permute-start(bf16[1,48,3072]{2,1,0:T(8,128)(2,1)} %pad_maximum_fusion.8), channel_id=1, source_target_pairs={{0,16},{8,24},{16,0},{24,8},{1,17},{9,25},{17,1},{25,9},{2,18},{10... | collective-permute-start | bytes 884744 | tf_op jit(solution)/shard_map/ppermute | solution.py:89
  80.4 8.0 %collective-permute-start.4 = (bf16[1,48,3072]{2,1,0:T(8,128)(2,1)}, bf16[1,48,3072]{2,1,0:T(8,128)(2,1)S(1)}, u32[]{:S(2)}, u32[]{:S(2)}) collective-permute-start(bf16[1,48,3072]{2,1,0:T(8,128)(2,1)} %pad_maximum_fusion.7), channel_id=1, source_target_pairs={{0,8},{8,16},{16,24},{24,0},{1,9},{9,17},{17,25},{25,1},{2,10},{10... | collective-permute-start | bytes 884744 | tf_op jit(solution)/shard_map/ppermute | solution.py:89
  88.4 1.9 collective-permute-start.5
  90.4 0.1 copy.9
  90.5 5.5 %collective-permute-done.3 = bf16[1,48,3072]{2,1,0:T(8,128)(2,1)S(1)} collective-permute-done((bf16[1,48,3072]{2,1,0:T(8,128)(2,1)}, bf16[1,48,3072]{2,1,0:T(8,128)(2,1)S(1)}, u32[]{:S(2)}, u32[]{:S(2)}) %collective-permute-start.3) | collective-permute-done | bytes 294944 | tf_op jit(solution)/shard_map/ppermute | solution.py:89
  96.0 40.9 %collective-permute-done.4 = bf16[1,48,3072]{2,1,0:T(8,128)(2,1)S(1)} collective-permute-done((bf16[1,48,3072]{2,1,0:T(8,128)(2,1)}, bf16[1,48,3072]{2,1,0:T(8,128)(2,1)S(1)}, u32[]{:S(2)}, u32[]{:S(2)}) %collective-permute-start.4) | collective-permute-done | bytes 294944 | tf_op jit(solution)/shard_map/ppermute | solution.py:89
  136.9 0.0 collective-permute-done.5
  136.9 1.1 pad_maximum_fusion.1
  138.1 0.0 all-gather.5.cloned.1.call-update
  138.1 68.7 %all_to_all.15 = bf16[16,96,384]{2,1,0:T(8,128)(2,1)S(1)} all-to-all(bf16[16,96,384]{2,1,0:T(8,128)(2,1)S(1)} %bitcast.14), channel_id=1, replica_groups=mesh['x'=4,'zlo'=4,'zhi'=4,'y'=4,'core'=2] {'zlo','zhi'}, dimensions={0} | all-to-all | bytes 2359296 | tf_op jit(solution)/shard_map/all_to_all | solution.py:130
  206.8 0.1 copy.10
  206.9 0.6 reshape.33.x_ref
  207.5 0.0 all-gather.3.cloned.1.call-done.refs_0_
  207.5 0.0 all-gather.5.cloned.1.call-done.refs_1_
  207.6 8.6 %shard_map.55 = bf16[192,3072]{1,0:T(8,128)(2,1)S(1)} custom-call(bf16[192,3072]{1,0:T(8,128)(2,1)S(1)} %reshape.33.x_ref, bf16[32,48,3072]{2,1,0:T(8,128)(2,1)} %all-gather.3.cloned.1.call-done.refs_0_, bf16[32,48,3072]{2,1,0:T(8,128)(2,1)} %all-gather.5.cloned.1.call-done.refs_1_), custom_call_target="tpu_custom_call" | custom-call | flops 3623878656 | bytes 21233664 | tf_op jit(solution)/shard_map/pallas_call | solution.py:54
  216.2 0.6 reshape.34
  216.8 71.7 %all_to_all.16 = bf16[64,24,384]{2,1,0:T(8,128)(2,1)S(1)} all-to-all(bf16[64,24,384]{2,1,0:T(8,128)(2,1)S(1)} %reshape.34), channel_id=1, replica_groups=mesh['x'=4,'zlo'=4,'zhi'=4,'y'=4,'core'=2] {'x','zlo','zhi'}, dimensions={0} | all-to-all | bytes 2359296 | tf_op jit(solution)/shard_map/all_to_all | solution.py:135
  288.4 0.6 reshape.35
  289.0 1.3 convolution_convert_fusion.1
  (2 shorter events, 0.0 us)
Async XLA Ops:
  6.5 29.6 %copy-start = (bf16[128,3072]{1,0:T(8,128)(2,1)S(1)}, bf16[128,3072]{1,0:T(8,128)(2,1)}, u32[]{:S(2)}) copy-start(bf16[128,3072]{1,0:T(8,128)(2,1)} %param.5) | copy-start | bytes 2359300
  6.5 2.1 copy-start.2
  6.5 2.1 copy-start.1
  8.8 26.9 %copy-start.4 = (s32[128,1]{0,1:T(1,128)S(1)}, s32[128,1]{0,1:T(1,128)}, u32[]{:S(2)}) copy-start(s32[128,1]{0,1:T(1,128)} %param.6) | copy-start | bytes 1540
  11.1 51.0 %collective-permute-start = (bf16[1,48,3072]{2,1,0:T(8,128)(2,1)}, bf16[1,48,3072]{2,1,0:T(8,128)(2,1)}, u32[]{:S(2)}, u32[]{:S(2)}) collective-permute-start(bf16[1,48,3072]{2,1,0:T(8,128)(2,1)} %pad_maximum_fusion.4), channel_id=1, source_target_pairs={{0,16},{8,24},{16,0},{24,8},{1,17},{9,25},{17,1},{25,9},{2,18},{10... | collective-permute-start | bytes 884744 | tf_op jit(solution)/shard_map/ppermute | solution.py:89
  25.9 36.1 %collective-permute-start.1 = (bf16[1,48,3072]{2,1,0:T(8,128)(2,1)}, bf16[1,48,3072]{2,1,0:T(8,128)(2,1)}, u32[]{:S(2)}, u32[]{:S(2)}) collective-permute-start(bf16[1,48,3072]{2,1,0:T(8,128)(2,1)} %pad_maximum_fusion.3), channel_id=1, source_target_pairs={{0,8},{8,16},{16,24},{24,0},{1,9},{9,17},{17,25},{25,1},{2,10},{10... | collective-permute-start | bytes 884744 | tf_op jit(solution)/shard_map/ppermute | solution.py:89
  30.2 41.2 %collective-permute-start.2 = (bf16[1,48,3072]{2,1,0:T(8,128)(2,1)}, bf16[1,48,3072]{2,1,0:T(8,128)(2,1)}, u32[]{:S(2)}, u32[]{:S(2)}) collective-permute-start(bf16[1,48,3072]{2,1,0:T(8,128)(2,1)} %pad_maximum_fusion.5), channel_id=1, source_target_pairs={{0,24},{8,0},{16,8},{24,16},{1,25},{9,1},{17,9},{25,17},{2,26},{10... | collective-permute-start | bytes 884744 | tf_op jit(solution)/shard_map/ppermute | solution.py:89
  38.0 35.7 %all-to-all-start = ((bf16[4,384,384]{2,1,0:T(8,128)(2,1)}), bf16[4,384,384]{2,1,0:T(8,128)(2,1)S(1)}, u32[]{:S(2)}, u32[]{:S(2)}) async-start(bf16[4,384,384]{2,1,0:T(8,128)(2,1)} %reshape.29), calls=%async_computation | async-start | bytes 2359296 | tf_op jit(solution)/shard_map/all_to_all | solution.py:121
  42.3 2.6 copy-start.3
  42.3 165.2 %all-gather.3.cloned.1.call-start = ((), (), s32[]{:S(2)}) async-start(), calls=%async_computation.3 | async-start | bytes 10616832 | tf_op jit(solution)/shard_map/all_gather | solution.py:106
  73.8 133.8 %all-gather.5.cloned.1.call-start = ((), (), s32[]{:S(2)}) async-start(), calls=%async_computation.4 | async-start | bytes 10616832 | tf_op jit(solution)/shard_map/all_gather | solution.py:106
  73.8 22.2 %collective-permute-start.3 = (bf16[1,48,3072]{2,1,0:T(8,128)(2,1)}, bf16[1,48,3072]{2,1,0:T(8,128)(2,1)S(1)}, u32[]{:S(2)}, u32[]{:S(2)}) collective-permute-start(bf16[1,48,3072]{2,1,0:T(8,128)(2,1)} %pad_maximum_fusion.8), channel_id=1, source_target_pairs={{0,16},{8,24},{16,0},{24,8},{1,17},{9,25},{17,1},{25,9},{2,18},{10... | collective-permute-start | bytes 884744 | tf_op jit(solution)/shard_map/ppermute | solution.py:89
  80.4 56.5 %collective-permute-start.4 = (bf16[1,48,3072]{2,1,0:T(8,128)(2,1)}, bf16[1,48,3072]{2,1,0:T(8,128)(2,1)S(1)}, u32[]{:S(2)}, u32[]{:S(2)}) collective-permute-start(bf16[1,48,3072]{2,1,0:T(8,128)(2,1)} %pad_maximum_fusion.7), channel_id=1, source_target_pairs={{0,8},{8,16},{16,24},{24,0},{1,9},{9,17},{17,25},{25,1},{2,10},{10... | collective-permute-start | bytes 884744 | tf_op jit(solution)/shard_map/ppermute | solution.py:89
  88.4 48.5 %collective-permute-start.5 = (bf16[1,48,3072]{2,1,0:T(8,128)(2,1)}, bf16[1,48,3072]{2,1,0:T(8,128)(2,1)S(1)}, u32[]{:S(2)}, u32[]{:S(2)}) collective-permute-start(bf16[1,48,3072]{2,1,0:T(8,128)(2,1)} %pad_maximum_fusion.9), channel_id=1, source_target_pairs={{0,24},{8,0},{16,8},{24,16},{1,25},{9,1},{17,9},{25,17},{2,26},{10... | collective-permute-start | bytes 884744 | tf_op jit(solution)/shard_map/ppermute | solution.py:89
Sparse Core Ops, SparseCore 0:
  73.9 65.7 all-gather.2
  141.8 62.0 all-gather.4
